TPU v7x, 256 devices: a whole 4x4x8 slice. The times are simulated.
256 devices in a mesh: gx: 8 (over z), gy: 4 (over x), gz: 8 (over y, core).
Axes of the slice: x: 4, y: 4, z: 8, core: 2. Of those that a mesh axis runs over, the one named last changes fastest.
Arguments:
- density: float32 [128, 128, 512], P('gz', 'gx', 'gy'), may hold values from 0.02 to 1, as said below
- volume_power_source: float32 [128, 128, 512], P('gz', 'gx', 'gy'), may hold values from -2.4 to 2.4
Outputs:
- thermal_solution: float32 [128, 128, 512], P('gz', 'gx', 'gy')
- filtered_sensitivity: float32 [128, 128, 512], P('gz', 'gx', 'gy')
Inputs may be any that keep to these rules, and one draw needn't show every extreme that they name: density of each cell, solid cells near one and void cells far lower.
All inputs are finite; a program needn't handle non-finite values.
Results may differ from a plain program's by a relative error of at most 0.00018.
Values sent between devices are 32-bit elements; how exact they have to be, the bound alone decides.
A program may use at most 64 MiB of HBM per device.

v0:
```python
import jax
import jax.numpy as jnp
from jax import lax
from jax.sharding import PartitionSpec as P

ITERS = 2


KMIN = 0.001
OMEGA = 0.8
FILTER_WEIGHT = 4.0


def with_halo(x, sides, width):
    for axis, dim in sides:
        size, length = (lax.axis_size(axis), x.shape[dim])
        up = [(i, (i + 1) % size) for i in range(size - 1)]
        down = [(j, i) for i, j in up]
        last = lax.slice_in_dim(x, length - width, length, axis=dim)
        first = lax.slice_in_dim(x, 0, width, axis=dim)
        before = lax.ppermute(last, axis, up)
        after = lax.ppermute(first, axis, down)
        x = jnp.concatenate([before, x, after], axis=dim)
    return x


def neighbour_sum(padded):
    total = padded[2:, 1:-1, 1:-1] + padded[:-2, 1:-1, 1:-1]
    total = total + padded[1:-1, 2:, 1:-1] + padded[1:-1, :-2, 1:-1]
    return total + padded[1:-1, 1:-1, 2:] + padded[1:-1, 1:-1, :-2]


def gap_squares(field, padded):
    total = jnp.zeros_like(field)
    for piece in (
        padded[2:, 1:-1, 1:-1],
        padded[:-2, 1:-1, 1:-1],
        padded[1:-1, 2:, 1:-1],
        padded[1:-1, :-2, 1:-1],
        padded[1:-1, 1:-1, 2:],
        padded[1:-1, 1:-1, :-2],
    ):
        total = total + (field - piece) ** 2
    return total


def fine_faces(field):
    return with_halo(field, (("gx", 1), ("gy", 2), ("gz", 0)), 1)


def latter_boundaries(field):
    return with_halo(field, (("gx", 1), ("gy", 2), ("gz", 0)), 1)


def coarse_faces(field):
    return with_halo(field, (("gx", 1), ("gy", 2), ("gz", 0)), 1)


def sum_rz_term(residual, precond):
    return lax.psum(jnp.sum(residual * precond), ("gx", "gy", "gz"))


def mirror_edges(padded, places):
    for dim, position, last_rank, cells in places:
        extent = padded.shape[dim]
        lower_rim = jnp.where(
            position == 0,
            lax.slice_in_dim(padded, 1, 2, axis=dim),
            lax.slice_in_dim(padded, 0, 1, axis=dim),
        )
        upper_rim = jnp.where(
            position == last_rank,
            lax.slice_in_dim(padded, extent - 2, extent - 1, axis=dim),
            lax.slice_in_dim(padded, extent - 1, extent, axis=dim),
        )
        padded = jnp.concatenate(
            [lower_rim, lax.slice_in_dim(padded, 1, extent - 1, axis=dim), upper_rim], axis=dim
        )
    return padded


def operator(field, field_pad, conduct, cond_pad, factor):
    return (
        factor
        * 0.5
        * (
            6.0 * conduct * field
            + field * neighbour_sum(cond_pad)
            - conduct * neighbour_sum(field_pad)
            - neighbour_sum(cond_pad * field_pad)
        )
    )


def block_sum(field):
    depth, rows, cols = field.shape
    return field.reshape(depth // 2, 2, rows // 2, 2, cols // 2, 2).sum(axis=(1, 3, 5))


def refine(field):
    return jnp.repeat(jnp.repeat(jnp.repeat(field, 2, axis=0), 2, axis=1), 2, axis=2)


def coarse_relax(coarse_rhs, coarse_cond, coarse_pad, diag_coarse, padder):
    correction = OMEGA * coarse_rhs / diag_coarse
    for sweep in range(3):
        image = operator(correction, padder(correction), coarse_cond, coarse_pad, 4.0)
        correction = correction + OMEGA * (coarse_rhs - image) / diag_coarse
    return correction


def local(density, volume_power_source):
    places = (
        (0, lax.axis_index("gz"), lax.axis_size("gz") - 1, density.shape[0]),
        (1, lax.axis_index("gx"), lax.axis_size("gx") - 1, density.shape[1]),
        (2, lax.axis_index("gy"), lax.axis_size("gy") - 1, density.shape[2]),
    )
    conduct = KMIN + (1.0 - KMIN) * density**3
    cond_pad = fine_faces(conduct)
    diag_fine = 0.5 * (6.0 * conduct + neighbour_sum(cond_pad))
    coarse_cond = block_sum(conduct) * 0.125
    coarse_pad = coarse_faces(coarse_cond)
    diag_coarse = 4.0 * 0.5 * (6.0 * coarse_cond + neighbour_sum(coarse_pad))

    def apply_fine(field):
        return operator(field, fine_faces(field), conduct, cond_pad, 1.0)

    def precondition(resid):
        smooth = OMEGA * resid / diag_fine
        coarse_rhs = block_sum(resid - apply_fine(smooth))
        correction = coarse_relax(coarse_rhs, coarse_cond, coarse_pad, diag_coarse, coarse_faces)
        smooth = smooth + refine(correction)
        return smooth + OMEGA * (resid - apply_fine(smooth)) / diag_fine

    thermal_solution = jnp.zeros_like(volume_power_source)
    residual = volume_power_source
    precond = precondition(residual)
    update_vector = precond
    rz_now = sum_rz_term(residual, precond)
    for step in range(ITERS):
        image = apply_fine(update_vector)
        update_scale = rz_now / lax.psum(jnp.sum(update_vector * image), ("gx", "gy", "gz"))
        thermal_solution = thermal_solution + update_scale * update_vector
        residual = residual - update_scale * image
        if step + 1 < ITERS:
            precond = precondition(residual)
            rz_next = sum_rz_term(residual, precond)
            update_vector = precond + rz_next / rz_now * update_vector
            rz_now = rz_next
    interface_gaps = gap_squares(thermal_solution, latter_boundaries(thermal_solution))
    sensitivity = -3.0 * (1.0 - KMIN) * density**2 * 0.5 * interface_gaps
    blurred_density = sensitivity
    for sweep in range(3):
        blurred_density = (
            sensitivity
            + FILTER_WEIGHT
            * neighbour_sum(mirror_edges(latter_boundaries(blurred_density), places))
        ) / (1.0 + 6.0 * FILTER_WEIGHT)
    return (thermal_solution, blurred_density)


def solution(mesh):
    placed = (P("gz", "gx", "gy"), P("gz", "gx", "gy"))
    return jax.shard_map(
        local,
        mesh=mesh,
        in_specs=placed,
        out_specs=(P("gz", "gx", "gy"), P("gz", "gx", "gy")),
        check_vma=False,
    )
```

profile of v0, /device:TPU:1, one launch (start us, length us, event | category | flops | bytes accessed | tf_op | source)
XLA Modules:
  0.0 733.3 jit_solution(2293381525319233291)
XLA Ops:
  1.6 9.8 %reshape.32 = f32[8,2,8,2,64,2]{5,4,3,2,1,0:T(8,128)} reshape(f32[16,16,128]{2,1,0:T(8,128)S(1)} %fusion.1) | data formatting | bytes 262144 | tf_op jit(solution)/shard_map/reshape | solution.py:97
  15.4 4.4 collective-permute-start.12
  21.1 4.2 collective-permute-start
  51.1 4.3 collective-permute-start.6
  61.1 4.2 collective-permute-start.8
  75.8 4.5 collective-permute-start.11
  81.7 9.8 %reshape.31 = f32[8,2,8,2,64,2]{5,4,3,2,1,0:T(8,128)} reshape(f32[16,16,128]{2,1,0:T(8,128)S(1)} %fusion.97) | data formatting | bytes 262144 | tf_op jit(solution)/shard_map/reshape | solution.py:97
  95.7 4.8 collective-permute-start.18
  101.9 4.5 collective-permute-done.19
  117.4 6.0 collective-permute-start.23
  124.6 4.8 collective-permute-start.24
  144.1 6.8 collective-permute-start.29
  168.7 7.1 collective-permute-start.35
  195.0 7.1 collective-permute-start.41
  220.7 7.1 collective-permute-start.47
  229.7 75.0 %all-reduce = (f32[]{:T(128)}, f32[]{:T(128)}) all-reduce(f32[]{:T(128)} %get-tuple-element.11, f32[]{:T(128)} %get-tuple-element.10), channel_id=1, replica_groups=mesh['gx'=8,'gy'=4,'gz'=8] {'gx','gy','gz'}, use_global_device_ids=true, to_apply=%region_3.0 | all-reduce | flops 2 | bytes 16 | tf_op jit(solution)/shard_map/psum | solution.py:60
  321.4 5.5 collective-permute-start.52
  330.5 9.8 %reshape.36 = f32[8,2,8,2,64,2]{5,4,3,2,1,0:T(8,128)} reshape(f32[16,16,128]{2,1,0:T(8,128)S(1)} %fusion.66) | data formatting | bytes 262144 | tf_op jit(solution)/shard_map/reshape | solution.py:97
  358.7 4.9 collective-permute-start.58
  368.6 4.4 collective-permute-start.60
  389.0 6.1 collective-permute-start.65
  413.0 7.1 collective-permute-start.71
  439.3 7.1 collective-permute-start.77
  448.3 73.6 %psum.30 = f32[]{:T(128)} all-reduce(f32[]{:T(128)} %get-tuple-element.14), channel_id=1, replica_groups=mesh['gx'=8,'gy'=4,'gz'=8] {'gx','gy','gz'}, use_global_device_ids=true, to_apply=%region_8.0 | all-reduce | flops 1 | bytes 8 | tf_op jit(solution)/shard_map/psum | solution.py:60
  538.6 5.6 collective-permute-start.82
  548.4 76.4 %psum.31 = f32[]{:T(128)} all-reduce(f32[]{:T(128)} %fusion.43), channel_id=1, replica_groups=mesh['gx'=8,'gy'=4,'gz'=8] {'gx','gy','gz'}, use_global_device_ids=true, to_apply=%region_10.0 | all-reduce | flops 1 | bytes 8 | tf_op jit(solution)/shard_map/psum | solution.py:142
  640.5 5.4 collective-permute-start.88
  665.6 4.7 collective-permute-start.94
  676.1 4.8 collective-permute-start.96
  699.3 4.5 collective-permute-start.101
  719.0 4.4 collective-permute-done.105
  725.9 4.8 collective-permute-start.107
  (402 shorter events, 332.9 us)
Async XLA Ops:
  15.4 11.2 %collective-permute-start.12 = (f32[8,1,64]{2,1,0:T(1,128)S(1)}, f32[8,1,64]{2,1,0:T(1,128)S(1)}, u32[]{:S(2)}, u32[]{:S(2)}) collective-permute-start(f32[8,1,64]{2,1,0:T(1,128)S(1)} %get-tuple-element.171), channel_id=1, source_target_pairs={{0,32},{32,64},{64,96},{96,128},{128,160},{160,192},{192,224},{1,3... | collective-permute-start | bytes 6152 | tf_op jit(solution)/shard_map/ppermute | solution.py:21
  21.1 10.0 %collective-permute-start = (f32[16,1,128]{2,0,1:T(8,128)S(1)}, f32[16,1,128]{2,0,1:T(8,128)S(1)}, u32[]{:S(2)}, u32[]{:S(2)}) collective-permute-start(f32[16,1,128]{2,0,1:T(8,128)S(1)} %bitcast.67), channel_id=1, source_target_pairs={{0,32},{32,64},{64,96},{96,128},{128,160},{160,192},{192,224},{1,3... | collective-permute-start | bytes 24584 | tf_op jit(solution)/shard_map/ppermute | solution.py:21
  26.7 9.9 %collective-permute-start.14 = (f32[8,10,1]{2,1,0:T(8,128)S(1)}, f32[8,10,1]{2,1,0:T(8,128)S(1)}, u32[]{:S(2)}, u32[]{:S(2)}) collective-permute-start(f32[8,10,1]{2,1,0:T(8,128)S(1)} %get-tuple-element.158), channel_id=1, source_target_pairs={{0,8},{8,16},{16,24},{1,9},{9,17},{17,25},{2,10},{10,18},{18,26},{... | collective-permute-start | bytes 968 | tf_op jit(solution)/shard_map/ppermute | solution.py:21
  31.4 12.6 %collective-permute-start.2 = (f32[16,18,1]{2,0,1:T(8,128)S(1)}, f32[16,18,1]{2,0,1:T(8,128)S(1)}, u32[]{:S(2)}, u32[]{:S(2)}) collective-permute-start(f32[16,18,1]{2,0,1:T(8,128)S(1)} %get-tuple-element.122), channel_id=1, source_target_pairs={{0,8},{8,16},{16,24},{1,9},{9,17},{17,25},{2,10},{10,18},{18,26},{... | collective-permute-start | bytes 3464 | tf_op jit(solution)/shard_map/ppermute | solution.py:21
  35.4 8.6 %collective-permute-start.3 = (f32[16,18,1]{2,0,1:T(8,128)S(1)}, f32[16,18,1]{2,0,1:T(8,128)S(1)}, u32[]{:S(2)}, u32[]{:S(2)}) collective-permute-start(f32[16,18,1]{2,0,1:T(8,128)S(1)} %get-tuple-element.121), channel_id=1, source_target_pairs={{8,0},{16,8},{24,16},{9,1},{17,9},{25,17},{10,2},{18,10},{26,18},{... | collective-permute-start | bytes 3464 | tf_op jit(solution)/shard_map/ppermute | solution.py:22
  36.8 58.8 %collective-permute-start.16 = (f32[1,10,66]{2,1,0:T(8,128)S(1)}, f32[1,10,66]{2,1,0:T(8,128)S(1)}, u32[]{:S(2)}, u32[]{:S(2)}) collective-permute-start(f32[1,10,66]{2,1,0:T(8,128)S(1)} %get-tuple-element.83), channel_id=1, source_target_pairs={{1,0},{2,1},{3,2},{4,3},{5,4},{6,5},{7,6},{9,8},{10,9},{11,10},{12... | collective-permute-start | bytes 7928 | tf_op jit(solution)/shard_map/ppermute | solution.py:22
  40.8 54.7 %collective-permute-start.17 = (f32[1,10,66]{2,1,0:T(8,128)S(1)}, f32[1,10,66]{2,1,0:T(8,128)S(1)}, u32[]{:S(2)}, u32[]{:S(2)}) collective-permute-start(f32[1,10,66]{2,1,0:T(8,128)S(1)} %get-tuple-element.84), channel_id=1, source_target_pairs={{0,1},{1,2},{2,3},{3,4},{4,5},{5,6},{6,7},{8,9},{9,10},{10,11},{11... | collective-permute-start | bytes 7928 | tf_op jit(solution)/shard_map/ppermute | solution.py:21
  61.1 7.6 %collective-permute-start.8 = (f32[16,18,1]{2,0,1:T(8,128)S(1)}, f32[16,18,1]{2,0,1:T(8,128)S(1)}, u32[]{:S(2)}, u32[]{:S(2)}) collective-permute-start(f32[16,18,1]{2,0,1:T(8,128)S(1)} %get-tuple-element.117), channel_id=1, source_target_pairs={{0,8},{8,16},{16,24},{1,9},{9,17},{17,25},{2,10},{10,18},{18,26},{... | collective-permute-start | bytes 3464 | tf_op jit(solution)/shard_map/ppermute | solution.py:21
  65.4 7.3 collective-permute-start.9
  73.1 7.5 %collective-permute-start.10 = (f32[1,18,130]{2,1,0:T(8,128)S(1)}, f32[1,18,130]{2,1,0:T(8,128)S(1)}, u32[]{:S(2)}, u32[]{:S(2)}) collective-permute-start(f32[1,18,130]{2,1,0:T(8,128)S(1)} %get-tuple-element.48), channel_id=1, source_target_pairs={{1,0},{2,1},{3,2},{4,3},{5,4},{6,5},{7,6},{9,8},{10,9},{11,10},{12... | collective-permute-start | bytes 28088 | tf_op jit(solution)/shard_map/ppermute | solution.py:22
  115.1 8.3 %collective-permute-start.22 = (f32[1,10,66]{2,1,0:T(8,128)S(1)}, f32[1,10,66]{2,1,0:T(8,128)S(1)}, u32[]{:S(2)}, u32[]{:S(2)}) collective-permute-start(f32[1,10,66]{2,1,0:T(8,128)S(1)} %get-tuple-element.82), channel_id=1, source_target_pairs={{1,0},{2,1},{3,2},{4,3},{5,4},{6,5},{7,6},{9,8},{10,9},{11,10},{12... | collective-permute-start | bytes 7928 | tf_op jit(solution)/shard_map/ppermute | solution.py:22
  142.1 8.7 %collective-permute-start.28 = (f32[1,10,66]{2,1,0:T(8,128)S(1)}, f32[1,10,66]{2,1,0:T(8,128)S(1)}, u32[]{:S(2)}, u32[]{:S(2)}) collective-permute-start(f32[1,10,66]{2,1,0:T(8,128)S(1)} %get-tuple-element.80), channel_id=1, source_target_pairs={{1,0},{2,1},{3,2},{4,3},{5,4},{6,5},{7,6},{9,8},{10,9},{11,10},{12... | collective-permute-start | bytes 7928 | tf_op jit(solution)/shard_map/ppermute | solution.py:22
  144.1 7.5 %collective-permute-start.29 = (f32[1,10,66]{2,1,0:T(8,128)S(1)}, f32[1,10,66]{2,1,0:T(8,128)S(1)}, u32[]{:S(2)}, u32[]{:S(2)}) collective-permute-start(f32[1,10,66]{2,1,0:T(8,128)S(1)} %get-tuple-element.79), channel_id=1, source_target_pairs={{0,1},{1,2},{2,3},{3,4},{4,5},{5,6},{6,7},{8,9},{9,10},{10,11},{11... | collective-permute-start | bytes 7928 | tf_op jit(solution)/shard_map/ppermute | solution.py:21
  166.8 9.0 %collective-permute-start.34 = (f32[1,10,66]{2,1,0:T(8,128)S(1)}, f32[1,10,66]{2,1,0:T(8,128)S(1)}, u32[]{:S(2)}, u32[]{:S(2)}) collective-permute-start(f32[1,10,66]{2,1,0:T(8,128)S(1)} %get-tuple-element.78), channel_id=1, source_target_pairs={{1,0},{2,1},{3,2},{4,3},{5,4},{6,5},{7,6},{9,8},{10,9},{11,10},{12... | collective-permute-start | bytes 7928 | tf_op jit(solution)/shard_map/ppermute | solution.py:22
  168.7 7.8 %collective-permute-start.35 = (f32[1,10,66]{2,1,0:T(8,128)S(1)}, f32[1,10,66]{2,1,0:T(8,128)S(1)}, u32[]{:S(2)}, u32[]{:S(2)}) collective-permute-start(f32[1,10,66]{2,1,0:T(8,128)S(1)} %get-tuple-element.77), channel_id=1, source_target_pairs={{0,1},{1,2},{2,3},{3,4},{4,5},{5,6},{6,7},{8,9},{9,10},{10,11},{11... | collective-permute-start | bytes 7928 | tf_op jit(solution)/shard_map/ppermute | solution.py:21
  193.1 9.2 %collective-permute-start.40 = (f32[1,18,130]{2,1,0:T(8,128)S(1)}, f32[1,18,130]{2,1,0:T(8,128)S(1)}, u32[]{:S(2)}, u32[]{:S(2)}) collective-permute-start(f32[1,18,130]{2,1,0:T(8,128)S(1)} %get-tuple-element.46), channel_id=1, source_target_pairs={{1,0},{2,1},{3,2},{4,3},{5,4},{6,5},{7,6},{9,8},{10,9},{11,10},{12... | collective-permute-start | bytes 28088 | tf_op jit(solution)/shard_map/ppermute | solution.py:22
  195.0 8.0 %collective-permute-start.41 = (f32[1,18,130]{2,1,0:T(8,128)S(1)}, f32[1,18,130]{2,1,0:T(8,128)S(1)}, u32[]{:S(2)}, u32[]{:S(2)}) collective-permute-start(f32[1,18,130]{2,1,0:T(8,128)S(1)} %get-tuple-element.45), channel_id=1, source_target_pairs={{0,1},{1,2},{2,3},{3,4},{4,5},{5,6},{6,7},{8,9},{9,10},{10,11},{11... | collective-permute-start | bytes 28088 | tf_op jit(solution)/shard_map/ppermute | solution.py:21
  218.7 9.2 %collective-permute-start.46 = (f32[1,18,130]{2,1,0:T(8,128)S(1)}, f32[1,18,130]{2,1,0:T(8,128)S(1)}, u32[]{:S(2)}, u32[]{:S(2)}) collective-permute-start(f32[1,18,130]{2,1,0:T(8,128)S(1)} %get-tuple-element.44), channel_id=1, source_target_pairs={{1,0},{2,1},{3,2},{4,3},{5,4},{6,5},{7,6},{9,8},{10,9},{11,10},{12... | collective-permute-start | bytes 28088 | tf_op jit(solution)/shard_map/ppermute | solution.py:22
  220.7 8.0 %collective-permute-start.47 = (f32[1,18,130]{2,1,0:T(8,128)S(1)}, f32[1,18,130]{2,1,0:T(8,128)S(1)}, u32[]{:S(2)}, u32[]{:S(2)}) collective-permute-start(f32[1,18,130]{2,1,0:T(8,128)S(1)} %get-tuple-element.43), channel_id=1, source_target_pairs={{0,1},{1,2},{2,3},{3,4},{4,5},{5,6},{6,7},{8,9},{9,10},{10,11},{11... | collective-permute-start | bytes 28088 | tf_op jit(solution)/shard_map/ppermute | solution.py:21
  321.4 7.9 %collective-permute-start.52 = (f32[1,18,130]{2,1,0:T(8,128)S(1)}, f32[1,18,130]{2,1,0:T(8,128)S(1)}, u32[]{:S(2)}, u32[]{:S(2)}) collective-permute-start(f32[1,18,130]{2,1,0:T(8,128)S(1)} %get-tuple-element.42), channel_id=1, source_target_pairs={{1,0},{2,1},{3,2},{4,3},{5,4},{6,5},{7,6},{9,8},{10,9},{11,10},{12... | collective-permute-start | bytes 28088 | tf_op jit(solution)/shard_map/ppermute | solution.py:22
  358.7 8.8 %collective-permute-start.58 = (f32[1,10,66]{2,1,0:T(8,128)S(1)}, f32[1,10,66]{2,1,0:T(8,128)S(1)}, u32[]{:S(2)}, u32[]{:S(2)}) collective-permute-start(f32[1,10,66]{2,1,0:T(8,128)S(1)} %get-tuple-element.76), channel_id=1, source_target_pairs={{1,0},{2,1},{3,2},{4,3},{5,4},{6,5},{7,6},{9,8},{10,9},{11,10},{12... | collective-permute-start | bytes 7928 | tf_op jit(solution)/shard_map/ppermute | solution.py:22
  386.7 8.4 %collective-permute-start.64 = (f32[1,10,66]{2,1,0:T(8,128)S(1)}, f32[1,10,66]{2,1,0:T(8,128)S(1)}, u32[]{:S(2)}, u32[]{:S(2)}) collective-permute-start(f32[1,10,66]{2,1,0:T(8,128)S(1)} %get-tuple-element.74), channel_id=1, source_target_pairs={{1,0},{2,1},{3,2},{4,3},{5,4},{6,5},{7,6},{9,8},{10,9},{11,10},{12... | collective-permute-start | bytes 7928 | tf_op jit(solution)/shard_map/ppermute | solution.py:22
  411.1 9.0 %collective-permute-start.70 = (f32[1,10,66]{2,1,0:T(8,128)S(1)}, f32[1,10,66]{2,1,0:T(8,128)S(1)}, u32[]{:S(2)}, u32[]{:S(2)}) collective-permute-start(f32[1,10,66]{2,1,0:T(8,128)S(1)} %get-tuple-element.72), channel_id=1, source_target_pairs={{1,0},{2,1},{3,2},{4,3},{5,4},{6,5},{7,6},{9,8},{10,9},{11,10},{12... | collective-permute-start | bytes 7928 | tf_op jit(solution)/shard_map/ppermute | solution.py:22
  413.0 7.8 %collective-permute-start.71 = (f32[1,10,66]{2,1,0:T(8,128)S(1)}, f32[1,10,66]{2,1,0:T(8,128)S(1)}, u32[]{:S(2)}, u32[]{:S(2)}) collective-permute-start(f32[1,10,66]{2,1,0:T(8,128)S(1)} %get-tuple-element.71), channel_id=1, source_target_pairs={{0,1},{1,2},{2,3},{3,4},{4,5},{5,6},{6,7},{8,9},{9,10},{10,11},{11... | collective-permute-start | bytes 7928 | tf_op jit(solution)/shard_map/ppermute | solution.py:21
  437.3 9.2 %collective-permute-start.76 = (f32[1,18,130]{2,1,0:T(8,128)S(1)}, f32[1,18,130]{2,1,0:T(8,128)S(1)}, u32[]{:S(2)}, u32[]{:S(2)}) collective-permute-start(f32[1,18,130]{2,1,0:T(8,128)S(1)} %get-tuple-element.40), channel_id=1, source_target_pairs={{1,0},{2,1},{3,2},{4,3},{5,4},{6,5},{7,6},{9,8},{10,9},{11,10},{12... | collective-permute-start | bytes 28088 | tf_op jit(solution)/shard_map/ppermute | solution.py:22
  439.3 8.0 %collective-permute-start.77 = (f32[1,18,130]{2,1,0:T(8,128)S(1)}, f32[1,18,130]{2,1,0:T(8,128)S(1)}, u32[]{:S(2)}, u32[]{:S(2)}) collective-permute-start(f32[1,18,130]{2,1,0:T(8,128)S(1)} %get-tuple-element.39), channel_id=1, source_target_pairs={{0,1},{1,2},{2,3},{3,4},{4,5},{5,6},{6,7},{8,9},{9,10},{10,11},{11... | collective-permute-start | bytes 28088 | tf_op jit(solution)/shard_map/ppermute | solution.py:21
  538.6 8.2 %collective-permute-start.82 = (f32[1,18,130]{2,1,0:T(8,128)S(1)}, f32[1,18,130]{2,1,0:T(8,128)S(1)}, u32[]{:S(2)}, u32[]{:S(2)}) collective-permute-start(f32[1,18,130]{2,1,0:T(8,128)S(1)} %get-tuple-element.38), channel_id=1, source_target_pairs={{1,0},{2,1},{3,2},{4,3},{5,4},{6,5},{7,6},{9,8},{10,9},{11,10},{12... | collective-permute-start | bytes 28088 | tf_op jit(solution)/shard_map/ppermute | solution.py:22
  640.5 7.7 %collective-permute-start.88 = (f32[1,18,130]{2,0,1:T(1,128)S(1)}, f32[1,18,130]{2,0,1:T(1,128)S(1)}, u32[]{:S(2)}, u32[]{:S(2)}) collective-permute-start(f32[1,18,130]{2,0,1:T(1,128)S(1)} %get-tuple-element.69), channel_id=1, source_target_pairs={{1,0},{2,1},{3,2},{4,3},{5,4},{6,5},{7,6},{9,8},{10,9},{11,10},{12... | collective-permute-start | bytes 28088 | tf_op jit(solution)/shard_map/ppermute | solution.py:22
  665.6 8.5 %collective-permute-start.94 = (f32[1,18,130]{2,0,1:T(1,128)S(1)}, f32[1,18,130]{2,0,1:T(1,128)S(1)}, u32[]{:S(2)}, u32[]{:S(2)}) collective-permute-start(f32[1,18,130]{2,0,1:T(1,128)S(1)} %get-tuple-element.67), channel_id=1, source_target_pairs={{1,0},{2,1},{3,2},{4,3},{5,4},{6,5},{7,6},{9,8},{10,9},{11,10},{12... | collective-permute-start | bytes 28088 | tf_op jit(solution)/shard_map/ppermute | solution.py:22
  689.0 7.7 %collective-permute-start.99 = (f32[16,18,1]{2,0,1:T(8,128)S(1)}, f32[16,18,1]{2,0,1:T(8,128)S(1)}, u32[]{:S(2)}, u32[]{:S(2)}) collective-permute-start(f32[16,18,1]{2,0,1:T(8,128)S(1)} %get-tuple-element.88), channel_id=1, source_target_pairs={{8,0},{16,8},{24,16},{9,1},{17,9},{25,17},{10,2},{18,10},{26,18},{... | collective-permute-start | bytes 3464 | tf_op jit(solution)/shard_map/ppermute | solution.py:22
  715.6 7.7 %collective-permute-start.105 = (f32[16,18,1]{2,0,1:T(8,128)S(1)}, f32[16,18,1]{2,0,1:T(8,128)S(1)}, u32[]{:S(2)}, u32[]{:S(2)}) collective-permute-start(f32[16,18,1]{2,0,1:T(8,128)S(1)} %get-tuple-element.86), channel_id=1, source_target_pairs={{8,0},{16,8},{24,16},{9,1},{17,9},{25,17},{10,2},{18,10},{26,18},{... | collective-permute-start | bytes 3464 | tf_op jit(solution)/shard_map/ppermute | solution.py:22
  723.6 7.1 collective-permute-start.106
  (79 other events, 568.4 us)
where the time goes:
time: 737 us; the launch traced here: 733 us
  starting transfers between devices  299 us (41%)
  blocking collectives  225 us (31%)
  waiting for transfers between devices  139 us (19%)
  local copies, waits for them, and re-layouts  36.1 us (5%)
  other arithmetic  26.8 us (4%)
    ppermute x54, starting transfers between devices, with_halo(): before = lax.ppermute(last, axis, up)  196 us
    psum x2, blocking collectives, sum_rz_term(): return lax.psum(jnp.sum(residual * precond), ('gx', 'gy', 'gz'))  149 us
    ppermute x54, waiting for transfers between devices, with_halo(): after = lax.ppermute(first, axis, down)  115 us
    ppermute x54, starting transfers between devices, with_halo(): after = lax.ppermute(first, axis, down)  103 us
    psum x1, blocking collectives, local(): lax.psum(jnp.sum(update_vector * image), ('gx', 'gy', 'gz'))  76.4 us
    reshape x3, local copies, waits for them, and re-layouts, block_sum(): field.reshape(depth // 2, 2, rows // 2, 2, cols // 2, 2).sum(axis=(1, 3, 5))  29.3 us
    ppermute x54, waiting for transfers between devices, with_halo(): before = lax.ppermute(last, axis, up)  24.7 us
  transfers between devices with their start and end apart: 108, of which 59 were waited for; matrix products, arithmetic and copies ran while one was open for 2% of the time, Pallas kernels for 0%

commit v1 on v0

v1 whole, which is shorter than its diff:
```python
import functools
import itertools

import jax
import jax.numpy as jnp
from jax import lax
from jax.experimental import pallas as pl
from jax.experimental.pallas import tpu as pltpu
from jax.sharding import PartitionSpec as P

KMIN = 0.001
OMEGA = 0.8
FILTER_WEIGHT = 4.0
MESH = pl.DeviceIdType.MESH
F32 = jnp.float32

LANES = 128
NZ = NX = 16
CZ = CX = 8
PAD = 8
FZ = NZ + 2 * PAD
CZP = CZ + 2 * PAD
LO, HI = 4, 28
WIN = HI - LO
CLO, CWIN = 4, 16

NEIGHBOURS = sorted(
    (o for o in itertools.product((-1, 0, 1), repeat=3) if o != (0, 0, 0)),
    key=lambda o: (sum(map(abs, o)), o),
)


def place(sizes, offset):
    dz, dx, dy = offset
    gx, gy, gz = sizes
    return (
        lax.rem(lax.axis_index("gx") + dx + gx, gx),
        lax.rem(lax.axis_index("gy") + dy + gy, gy),
        lax.rem(lax.axis_index("gz") + dz + gz, gz),
    )


def other_core():
    gz = lax.axis_index("gz")
    return gz + 1 - 2 * lax.rem(gz, 2)


def lane_iota(rows):
    return lax.broadcasted_iota(jnp.int32, (rows, LANES), 1)


def lane_neighbours(main, side, step):
    lane = lane_iota(main.shape[0])
    up_main, up_side = pltpu.roll(main, LANES - step, 1), pltpu.roll(side, LANES - step, 1)
    dn_main, dn_side = pltpu.roll(main, step, 1), pltpu.roll(side, step, 1)
    last, first = lane >= LANES - step, lane < step
    ahead = (jnp.where(last, up_side, up_main), jnp.where(last, up_main, up_side))
    behind = (jnp.where(first, dn_side, dn_main), jnp.where(first, dn_main, dn_side))
    return ahead, behind


def pair_lanes(v):
    even = lax.rem(lane_iota(v.shape[0]), 2) == 0
    return v + jnp.where(even, pltpu.roll(v, LANES - 1, 1), pltpu.roll(v, 1, 1))


def loop(lower, upper, body):
    lax.fori_loop(lower, upper, lambda i, c: (body(i), c)[1], 0)


class Exchange:
    def __init__(self, sizes, arr, fields, halo, n, group, pks, pkr, ssem, rsem):
        self.sizes, self.arr, self.fields, self.halo, self.n = sizes, arr, fields, halo, n
        self.group = group
        self.per = LANES // group
        self.pks, self.pkr, self.ssem, self.rsem = pks, pkr, ssem, rsem
        self.copies = []

    def pack(self):
        per, group, n = self.per, self.group, self.n
        lane = lane_iota(n)
        for f in range(self.fields):
            for g in range(n // per):
                acc = None
                for k in range(per):
                    v = self.arr[f, 0, PAD + g * per + k, PAD : PAD + n, :]
                    v = pltpu.roll(v, group * k + group // 2, 1)
                    acc = v if acc is None else jnp.where(lane >= group * k, v, acc)
                self.pks[f, g] = acc

    def start(self):
        n, h, per = self.n, self.halo, self.per
        groups = n // per
        side_groups = -(-h // per)
        for i, (dz, dx, dy) in enumerate(NEIGHBOURS):
            rows = {0: (0, n, PAD), 1: (n - PAD, PAD, 0), -1: (0, PAD, PAD + n)}[dx]
            if dy == 0:
                planes = {0: (0, n, PAD), 1: (n - h, h, PAD - h), -1: (0, h, PAD + n)}[dz]
                src = self.arr.at[:, 0, pl.ds(PAD + planes[0], planes[1]), pl.ds(PAD + rows[0], rows[1]), :]
                dst = self.arr.at[:, 0, pl.ds(planes[2], planes[1]), pl.ds(rows[2], rows[1]), :]
            else:
                first = PAD // per
                s = side_groups
                gr = {0: (0, groups, first), 1: (groups - s, s, first - s), -1: (0, s, first + groups)}[dz]
                src = self.pks.at[:, pl.ds(gr[0], gr[1]), pl.ds(rows[0], rows[1]), :]
                dst = self.pkr.at[0 if dy == 1 else 1, :, pl.ds(gr[2], gr[1]), pl.ds(rows[2], rows[1]), :]
            cp = pltpu.make_async_remote_copy(
                src_ref=src,
                dst_ref=dst,
                send_sem=self.ssem.at[i],
                recv_sem=self.rsem.at[i],
                device_id=place(self.sizes, (dz, dx, dy)),
                device_id_type=MESH,
            )
            cp.start()
            self.copies.append(cp)

    def wait(self):
        for cp in self.copies:
            cp.wait_recv()

    def unpack(self):
        per, group, n, h = self.per, self.group, self.n, self.halo
        rows = n + 2 * PAD
        low = lax.rem(lane_iota(rows), group) < group // 2

        def body(g):
            for f in range(self.fields):
                merged = jnp.where(low, self.pkr[0, f, g], self.pkr[1, f, g])
                for k in range(per):
                    self.arr[f, 1, g * per + k, 0:rows, :] = pltpu.roll(
                        merged, LANES - group * k - group // 2, 1
                    )

        first = (PAD - h) // per
        last = -(-(PAD + n + h) // per)
        loop(first, last, body)

    def finish(self):
        for cp in self.copies:
            cp.wait_send()


def kernel(
    sizes,
    rho_ref,
    src_ref,
    out_t,
    out_f,
    fin,
    cond,
    kzm,
    kx,
    kyp,
    kym,
    diag,
    inv,
    zpre,
    vv,
    z0,
    q0,
    last,
    ww,
    mask,
    cin,
    cin2,
    cc,
    kcz,
    kcx,
    kcyp,
    kcym,
    cinv,
    ea,
    eb,
    cmask,
    refined,
    tmp,
    pks1,
    pkr1,
    pks2,
    pkr2,
    pks3,
    pkr3,
    pks4,
    pkr4,
    red1,
    red2,
    ssems,
    rsems,
    rs1,
    rr1,
    rs2,
    rr2,
):
    gxs, gys, gzs = sizes
    gx, gy, gz = lax.axis_index("gx"), lax.axis_index("gy"), lax.axis_index("gz")

    def peer1(dy, dz):
        return (gx, lax.rem(gy + dy, gys), lax.rem(gz + 2 * dz, gzs))

    def peer2(dx, flip):
        return (lax.rem(gx + dx, gxs), gy, other_core() if flip else gz)

    group1 = [(dy, dz) for dy in range(gys) for dz in range(gzs // 2) if (dy, dz) != (0, 0)]
    group2 = [(dx, fl) for dx in range(gxs) for fl in range(2) if (dx, fl) != (0, 0)]

    barrier = pltpu.get_barrier_semaphore()
    partners = [place(sizes, o) for o in NEIGHBOURS]
    partners += [peer1(*o) for o in group1 if o not in ((1, 0), (gys - 1, 0))]
    partners += [peer2(*o) for o in group2 if o[0] not in (0, 1, gxs - 1)]
    for device in partners:
        pl.semaphore_signal(barrier, inc=1, device_id=device, device_id_type=MESH)

    fin[0, 0, PAD : PAD + NZ, PAD : PAD + NX, :] = rho_ref[...]
    fin[1, 0, PAD : PAD + NZ, PAD : PAD + NX, :] = src_ref[...]
    ex1 = Exchange(sizes, fin, 2, 5, NZ, 16, pks1, pkr1, ssems.at[0], rsems.at[0])
    ex1.pack()

    row = lax.broadcasted_iota(jnp.int32, (FZ, LANES), 0) - PAD + gx * NX
    lane = lane_iota(FZ)
    row_in = (row >= 0) & (row < gxs * NX)
    left, right = gy > 0, gy < gys - 1
    right_end = jnp.where(right, 8, 0)
    left_start = jnp.where(left, LANES - 8, LANES)
    side_in = row_in & ((lane < right_end) | (lane >= left_start))
    mask[0] = jnp.where(row_in, 1.0, 0.0)
    mask[1] = jnp.where(side_in, 1.0, 0.0)
    crow = lax.broadcasted_iota(jnp.int32, (24, LANES), 0) - PAD + gx * CX
    clane = lane_iota(24)
    crow_in = (crow >= 0) & (crow < gxs * CX)
    cside_in = crow_in & (
        (clane < jnp.where(right, 16, 0)) | (clane >= jnp.where(left, LANES - 16, LANES))
    )
    cmask[0] = jnp.where(crow_in, 1.0, 0.0)
    cmask[1] = jnp.where(cside_in, 1.0, 0.0)

    def plane_in(z, cells):
        g = gz * cells + z - PAD
        return jnp.where((g >= 0) & (g < gzs * cells), 1.0, 0.0).astype(F32)

    pl.semaphore_wait(barrier, len(partners))
    ex1.start()
    ex1.wait()
    ex1.unpack()

    def conductivity(z):
        inside = plane_in(z, NZ)
        for s in range(2):
            r = fin[0, s, z]
            cond[s, z, 0:FZ, :] = (mask[s] * inside) * (KMIN + (1.0 - KMIN) * (r * r * r))

    loop(3, 29, conductivity)

    def faces(z):
        here = [cond[s, z, LO:HI, :] for s in range(2)]
        ahead, behind = lane_neighbours(here[0], here[1], 1)
        inside = plane_in(z, NZ)
        for s in range(2):
            c = here[s]
            zm = 0.5 * (cond[s, z - 1, LO:HI, :] + c)
            zp = 0.5 * (cond[s, z + 1, LO:HI, :] + c)
            xp = 0.5 * (cond[s, z, LO + 1 : HI + 1, :] + c)
            xm = 0.5 * (cond[s, z, LO - 1 : HI - 1, :] + c)
            yp = 0.5 * (ahead[s] + c)
            ym = 0.5 * (behind[s] + c)
            d = (zm + zp) + (xp + xm) + (yp + ym)
            kzm[s, z, LO:HI, :] = zm
            kx[s, z, LO:HI, :] = xp
            kx[s, z, LO - 1 : LO, :] = xm[0:1, :]
            kyp[s, z, LO:HI, :] = yp
            kym[s, z, LO:HI, :] = ym
            diag[s, z, LO:HI, :] = d
            ok = mask[s, LO:HI, :] * inside > 0.5
            i = jnp.where(ok, OMEGA / d, 0.0)
            inv[s, z, LO:HI, :] = i
            zpre[s, z, LO:HI, :] = i * fin[1, s, z, LO:HI, :]

    loop(4, 28, faces)

    def off_diagonal(field, z, lo, n, sides):
        here = [field[s, z, lo : lo + n, :] for s in range(2)]
        ahead, behind = lane_neighbours(here[0], here[1], 1)
        out = []
        for s in range(sides):
            t = kzm[s, z, lo : lo + n, :] * field[s, z - 1, lo : lo + n, :]
            t = t + kzm[s, z + 1, lo : lo + n, :] * field[s, z + 1, lo : lo + n, :]
            u = kx[s, z, lo : lo + n, :] * field[s, z, lo + 1 : lo + n + 1, :]
            u = u + kx[s, z, lo - 1 : lo + n - 1, :] * field[s, z, lo - 1 : lo + n - 1, :]
            v = kyp[s, z, lo : lo + n, :] * ahead[s] + kym[s, z, lo : lo + n, :] * behind[s]
            out.append((t + u) + v)
        return out

    def coarse_rhs(load, field, dest):
        def body(k):
            total = None
            for j in range(2):
                z = PAD + 2 * k + j
                t = (1.0 - OMEGA) * load(z) + off_diagonal(field, z, PAD, NX, 1)[0]
                total = t if total is None else total + t
            tmp[k, 0, 0:NX, :] = pair_lanes(total)
            dest[0, 0, PAD + k, PAD : PAD + CX, :] = (
                tmp[k, 0, pl.ds(0, CX, 2), :] + tmp[k, 0, pl.ds(1, CX, 2), :]
            )

        loop(0, CZ, body)

    coarse_rhs(lambda z: fin[1, 0, z, PAD : PAD + NX, :], zpre, cin)

    def coarse_cond(vc):
        z = 2 * vc - PAD
        for s in range(2):
            u = cond[s, z, 0:FZ, :] + cond[s, z + 1, 0:FZ, :]
            refined[vc, s] = pair_lanes(u)
            cc[s, vc, 4:20, :] = 0.125 * (
                refined[vc, s, pl.ds(0, 16, 2), :] + refined[vc, s, pl.ds(1, 16, 2), :]
            )

    loop(7, 17, coarse_cond)

    def coarse_diag(vc):
        c = cc[0, vc, 8:16, :]
        ahead, behind = lane_neighbours(c, cc[1, vc, 8:16, :], 2)
        t = cc[0, vc - 1, 8:16, :] + cc[0, vc + 1, 8:16, :]
        t = t + (cc[0, vc, 7:15, :] + cc[0, vc, 9:17, :])
        t = t + (ahead[0] + behind[0])
        cin[1, 0, vc, 8:16, :] = c
        cin[2, 0, vc, 8:16, :] = OMEGA / (2.0 * (6.0 * c + t))

    loop(8, 16, coarse_diag)

    ex2 = Exchange(sizes, cin, 3, 5, CZ, 32, pks2, pkr2, ssems.at[1], rsems.at[1])
    ex2.pack()
    ex2.start()
    ex2.wait()
    ex2.unpack()

    def coarse_masked(vc):
        inside = plane_in(vc, CZ)
        for s in range(2):
            ok = cmask[s] * inside > 0.5
            cc[s, vc, 0:24, :] = jnp.where(ok, cin[1, s, vc, 0:24, :], 0.0)
            i = jnp.where(ok, cin[2, s, vc, 0:24, :], 0.0)
            cinv[s, vc, 0:24, :] = i
            ea[s, vc, 0:24, :] = i * cin[0, s, vc, 0:24, :]

    loop(3, 21, coarse_masked)

    def coarse_faces(vc):
        lo, hi = CLO, CLO + CWIN
        here = [cc[s, vc, lo:hi, :] for s in range(2)]
        ahead, behind = lane_neighbours(here[0], here[1], 2)
        for s in range(2):
            c = here[s]
            kcz[s, vc, lo:hi, :] = 2.0 * (c + cc[s, vc - 1, lo:hi, :])
            kcx[s, vc, lo:hi, :] = 2.0 * (c + cc[s, vc, lo + 1 : hi + 1, :])
            kcx[s, vc, lo - 1 : lo, :] = 2.0 * (c[0:1, :] + cc[s, vc, lo - 1 : lo, :])
            kcyp[s, vc, lo:hi, :] = 2.0 * (c + ahead[s])
            kcym[s, vc, lo:hi, :] = 2.0 * (c + behind[s])

    loop(4, 21, coarse_faces)

    def sweep(e, e_next, rhs, first, end):
        lo, hi = CLO, CLO + CWIN

        def body(vc):
            here = [e[s, vc, lo:hi, :] for s in range(2)]
            ahead, behind = lane_neighbours(here[0], here[1], 2)
            for s in range(2):
                t = kcz[s, vc, lo:hi, :] * e[s, vc - 1, lo:hi, :]
                t = t + kcz[s, vc + 1, lo:hi, :] * e[s, vc + 1, lo:hi, :]
                u = kcx[s, vc, lo:hi, :] * e[s, vc, lo + 1 : hi + 1, :]
                u = u + kcx[s, vc, lo - 1 : hi - 1, :] * e[s, vc, lo - 1 : hi - 1, :]
                v = kcyp[s, vc, lo:hi, :] * ahead[s] + kcym[s, vc, lo:hi, :] * behind[s]
                r = rhs[0, s, vc, lo:hi, :] + ((t + u) + v)
                e_next[s, vc, lo:hi, :] = (1.0 - OMEGA) * here[s] + cinv[s, vc, lo:hi, :] * r

        loop(first, end, body)

    def add_refined(e, base, first, end):
        def body(vc):
            for s in range(2):
                v = e[s, vc, CLO : CLO + CWIN, :]
                refined[vc, s, pl.ds(0, CWIN, 2), :] = v
                refined[vc, s, pl.ds(1, CWIN, 2), :] = v
                fine = refined[vc, s, LO:HI, :]
                for j in range(2):
                    z = 2 * vc - PAD + j
                    vv[s, z, LO:HI, :] = base[s, z, LO:HI, :] + fine

        loop(first, end, body)

    sweep(ea, eb, cin, 4, 20)
    sweep(eb, ea, cin, 5, 19)
    sweep(ea, eb, cin, 6, 18)
    add_refined(eb, zpre, 6, 18)

    def post(z):
        b = off_diagonal(vv, z, LO, WIN, 2)
        for s in range(2):
            z0[s, z, LO:HI, :] = (1.0 - OMEGA) * vv[s, z, LO:HI, :] + inv[s, z, LO:HI, :] * (
                fin[1, s, z, LO:HI, :] + b[s]
            )

    loop(5, 27, post)

    def image(z):
        b = off_diagonal(z0, z, LO, WIN, 2)
        for s in range(2):
            q = diag[s, z, LO:HI, :] * z0[s, z, LO:HI, :] - b[s]
            q0[s, z, LO:HI, :] = q
            zpre[s, z, LO:HI, :] = inv[s, z, LO:HI, :] * q

    loop(6, 26, image)

    coarse_rhs(lambda z: q0[0, z, PAD : PAD + NX, :], zpre, cin2)
    ex3 = Exchange(sizes, cin2, 1, 4, CZ, 32, pks3, pkr3, ssems.at[2], rsems.at[2])
    ex3.pack()
    ex3.start()
    ex3.wait()
    ex3.unpack()

    def first_correction(vc):
        for s in range(2):
            ea[s, vc, 0:24, :] = cinv[s, vc, 0:24, :] * cin2[0, s, vc, 0:24, :]

    loop(4, 20, first_correction)
    sweep(ea, eb, cin2, 5, 19)
    sweep(eb, ea, cin2, 6, 18)
    sweep(ea, eb, cin2, 7, 17)
    add_refined(eb, zpre, 7, 17)

    def post_second(z):
        b = off_diagonal(vv, z, LO, WIN, 2)
        for s in range(2):
            ww[s, z, LO:HI, :] = (1.0 - OMEGA) * vv[s, z, LO:HI, :] + inv[s, z, LO:HI, :] * (
                q0[s, z, LO:HI, :] + b[s]
            )

    loop(7, 25, post_second)

    own = slice(PAD, PAD + NX)

    def dots(z, acc):
        w = ww[0, z, own, :]
        zz = z0[0, z, own, :]
        q = q0[0, z, own, :]
        r = fin[1, 0, z, own, :]
        p = diag[0, z, own, :] * w - off_diagonal(ww, z, PAD, NX, 1)[0]
        last[0, 0, z, own, :] = zz
        last[1, 0, z, own, :] = w
        terms = (r * zz, zz * q, r * w, q * w, zz * p, w * p)
        return tuple(a + t[0:8] + t[8:16] for a, t in zip(acc, terms))

    zero = jnp.zeros((8, LANES), F32)
    acc = lax.fori_loop(PAD, PAD + NZ, dots, (zero,) * 6)
    which = lax.broadcasted_iota(jnp.int32, (8, LANES), 0)
    part = zero
    for i, a in enumerate(acc):
        part = jnp.where(which == i, jnp.sum(a, axis=0, keepdims=True), part)

    rank1 = gy * (gzs // 2) + gz // 2
    red1[rank1] = part
    cps1 = []
    for i, o in enumerate(group1):
        cp = pltpu.make_async_remote_copy(
            src_ref=red1.at[rank1],
            dst_ref=red1.at[rank1],
            send_sem=rs1.at[i],
            recv_sem=rr1.at[i],
            device_id=peer1(*o),
            device_id_type=MESH,
        )
        cp.start()
        cps1.append(cp)
    ex4 = Exchange(sizes, last, 2, 4, NZ, 16, pks4, pkr4, ssems.at[3], rsems.at[3])
    ex4.pack()
    ex4.start()
    for cp in cps1:
        cp.wait_recv()
    part = red1[0]
    for i in range(1, len(group1) + 1):
        part = part + red1[i]
    rank2 = gx * 2 + lax.rem(gz, 2)
    red2[rank2] = part
    cps2 = []
    for i, o in enumerate(group2):
        cp = pltpu.make_async_remote_copy(
            src_ref=red2.at[rank2],
            dst_ref=red2.at[rank2],
            send_sem=rs2.at[i],
            recv_sem=rr2.at[i],
            device_id=peer2(*o),
            device_id_type=MESH,
        )
        cp.start()
        cps2.append(cp)
    ex4.wait()
    ex4.unpack()
    for cp in cps2:
        cp.wait_recv()
    total = red2[0]
    for i in range(1, len(group2) + 1):
        total = total + red2[i]
    total = jnp.broadcast_to(jnp.sum(total, axis=1, keepdims=True), (8, LANES))
    rz, zq, rw, qw, zp, wp = (total[i : i + 1, :] for i in range(6))
    a0 = rz / zq
    rz1 = a0 * (a0 * qw - rw)
    beta = rz1 / rz
    gamma = 1.0 + beta
    a1 = rz1 / (gamma * gamma * zq - a0 * gamma * (zp + qw) + a0 * a0 * wp)
    c1 = jnp.broadcast_to(a0 + a1 * gamma, (WIN, LANES))
    c2 = jnp.broadcast_to(-a1 * a0, (WIN, LANES))

    def solution_plane(z):
        inside = plane_in(z, NZ)
        for s in range(2):
            x = c1 * last[0, s, z, LO:HI, :] + c2 * last[1, s, z, LO:HI, :]
            vv[s, z, LO:HI, :] = x * (mask[s, LO:HI, :] * inside)

    loop(4, 28, solution_plane)

    def copy_out(z):
        out_t[z] = vv[0, z + PAD, own, :]

    loop(0, NZ, copy_out)

    def sensitivity(z):
        here = [vv[s, z, LO:HI, :] for s in range(2)]
        ahead, behind = lane_neighbours(here[0], here[1], 1)
        inside = plane_in(z, NZ)
        for s in range(2):
            x = here[s]
            g = (x - vv[s, z - 1, LO:HI, :]) ** 2 + (x - vv[s, z + 1, LO:HI, :]) ** 2
            g = g + (x - vv[s, z, LO - 1 : HI - 1, :]) ** 2
            g = g + (x - vv[s, z, LO + 1 : HI + 1, :]) ** 2
            g = g + ((x - ahead[s]) ** 2 + (x - behind[s]) ** 2)
            r = fin[0, s, z, LO:HI, :] * (mask[s, LO:HI, :] * inside)
            v = (-3.0 * (1.0 - KMIN) * 0.5) * (r * r) * g
            z0[s, z, LO:HI, :] = v
            ww[s, z, LO:HI, :] = v * (1.0 / (1.0 + 6.0 * FILTER_WEIGHT))

    loop(5, 27, sensitivity)

    wlane = lane_iota(WIN)
    wrow = lax.broadcasted_iota(jnp.int32, (WIN, LANES), 0) + LO - PAD + gx * NX
    outside_row = jnp.where(wrow == 0, 1.0, 0.0) + jnp.where(wrow == gxs * NX - 1, 1.0, 0.0)
    outside_main = outside_row + jnp.where((wlane == 0) & (gy == 0), 1.0, 0.0)
    outside_main = outside_main + jnp.where((wlane == LANES - 1) & (gy == gys - 1), 1.0, 0.0)
    outside = (outside_main, outside_row)
    weight = FILTER_WEIGHT / (1.0 + 6.0 * FILTER_WEIGHT)

    def blur(f, f_next, first, end):
        def body(z):
            here = [f[s, z, LO:HI, :] for s in range(2)]
            ahead, behind = lane_neighbours(here[0], here[1], 1)
            inside = plane_in(z, NZ)
            g = gz * NZ + z - PAD
            ends = jnp.where((g == 0) | (g == gzs * NZ - 1), 1.0, 0.0).astype(F32)
            for s in range(2):
                t = f[s, z - 1, LO:HI, :] + f[s, z + 1, LO:HI, :]
                t = t + (f[s, z, LO - 1 : HI - 1, :] + f[s, z, LO + 1 : HI + 1, :])
                t = t + (ahead[s] + behind[s])
                t = t + (outside[s] + ends) * here[s]
                f_next[s, z, LO:HI, :] = ww[s, z, LO:HI, :] + t * (
                    mask[s, LO:HI, :] * (inside * weight)
                )

        loop(first, end, body)

    blur(z0, q0, 6, 26)
    blur(q0, z0, 7, 25)

    def blur_out(k):
        z = k + PAD
        f = z0
        here = [f[s, z, own, :] for s in range(2)]
        ahead, behind = lane_neighbours(here[0], here[1], 1)
        g = gz * NZ + k
        ends = jnp.where((g == 0) | (g == gzs * NZ - 1), 1.0, 0.0).astype(F32)
        t = f[0, z - 1, own, :] + f[0, z + 1, own, :]
        t = t + (f[0, z, PAD - 1 : PAD + NX - 1, :] + f[0, z, PAD + 1 : PAD + NX + 1, :])
        t = t + (ahead[0] + behind[0])
        t = t + (outside[0][PAD - LO : PAD - LO + NX] + ends) * here[0]
        out_f[k] = ww[0, z, own, :] + t * weight

    loop(0, NZ, blur_out)

    for ex in (ex1, ex2, ex3, ex4):
        ex.finish()
    for cp in cps1 + cps2:
        cp.wait_send()


def local(sizes, density, volume_power_source):
    shape = jax.ShapeDtypeStruct((NZ, NX, LANES), F32)
    vmem = pl.BlockSpec(memory_space=pltpu.VMEM)

    def fine(*lead, rows=FZ):
        return pltpu.VMEM((*lead, 2, FZ, rows, LANES), F32)

    def coarse(*lead):
        return pltpu.VMEM((*lead, 2, CZP, 32, LANES), F32)

    n = len(NEIGHBOURS)
    g1 = sizes[1] * (sizes[2] // 2)
    g2 = sizes[0] * 2
    scratch = [
        fine(2),
        fine(rows=40),
        *[fine() for _ in range(10)],
        fine(2),
        fine(),
        pltpu.VMEM((2, FZ, LANES), F32),
        coarse(3),
        coarse(1),
        *[coarse() for _ in range(8)],
        pltpu.VMEM((2, 24, LANES), F32),
        pltpu.VMEM((CZP, 2, FZ, LANES), F32),
        pltpu.VMEM((CZ, 1, NX, LANES), F32),
        pltpu.VMEM((2, 2, NX, LANES), F32),
        pltpu.VMEM((2, 2, 4, FZ, LANES), F32),
        pltpu.VMEM((3, 2, CX, LANES), F32),
        pltpu.VMEM((2, 3, 6, 24, LANES), F32),
        pltpu.VMEM((1, 2, CX, LANES), F32),
        pltpu.VMEM((2, 1, 6, 24, LANES), F32),
        pltpu.VMEM((2, 2, NX, LANES), F32),
        pltpu.VMEM((2, 2, 4, FZ, LANES), F32),
        pltpu.VMEM((g1, 8, LANES), F32),
        pltpu.VMEM((g2, 8, LANES), F32),
        pltpu.SemaphoreType.DMA((4, n)),
        pltpu.SemaphoreType.DMA((4, n)),
        pltpu.SemaphoreType.DMA((g1 - 1,)),
        pltpu.SemaphoreType.DMA((g1 - 1,)),
        pltpu.SemaphoreType.DMA((g2 - 1,)),
        pltpu.SemaphoreType.DMA((g2 - 1,)),
    ]
    return pl.pallas_call(
        functools.partial(kernel, sizes),
        out_shape=(shape, shape),
        in_specs=[vmem, vmem],
        out_specs=(vmem, vmem),
        scratch_shapes=scratch,
        compiler_params=pltpu.CompilerParams(
            collective_id=0, has_side_effects=True, vmem_limit_bytes=48 * 1024 * 1024
        ),
        name="heat_sink_step",
    )(density, volume_power_source)


def solution(mesh):
    sizes = tuple(mesh.shape[a] for a in ("gx", "gy", "gz"))
    spec = P("gz", "gx", "gy")
    return jax.shard_map(
        functools.partial(local, sizes),
        mesh=mesh,
        in_specs=(spec, spec),
        out_specs=(spec, spec),
        check_vma=False,
    )
```

time: 737 us -> 85.1 us (0.12)
  starting transfers between devices: 299 us -> 0 us
  blocking collectives: 225 us -> 0 us
  waiting for transfers between devices: 139 us -> 0 us
  Pallas kernels: 0 us -> 81.2 us
  local copies, waits for them, and re-layouts: 36.1 us -> 3.11 us
  other arithmetic: 26.8 us -> 0 us
    ppermute x108 -> x0, starting transfers between devices: 299 us -> none  [the longest x54 196 us: with_halo(): before = lax.ppermute(last, axis, up)]
    psum x3 -> x0, blocking collectives: 225 us -> none  [the longest x2 149 us: sum_rz_term(): return lax.psum(jnp.sum(residual * precond), ('gx', 'gy', 'gz'))]
    ppermute x108 -> x0, waiting for transfers between devices: 139 us -> none  [the longest x54 115 us: with_halo(): after = lax.ppermute(first, axis, down)]
    pallas_call x0 -> x1, Pallas kernels: none -> 81.2 us  [local(): pl.pallas_call(functools.partial(kernel, sizes), out_shape=(shape, shape)...]
    reshape x7 -> x0, local copies, waits for them, and re-layouts: 30.7 us -> none  [the longest x3 29.3 us: block_sum(): field.reshape(depth // 2, 2, rows // 2, 2, cols // 2, 2).sum(axis=(1, 3, 5))]
    reduce_sum x6 -> x0, other arithmetic: 15 us -> none  [the longest x3 12.1 us: block_sum(): field.reshape(depth // 2, 2, rows // 2, 2, cols // 2, 2).sum(axis=(1, 3, 5))]
  transfers between devices with their start and end apart: 108 -> 0, of which waited for: 59 -> 0; matrix products, arithmetic and copies ran while one was open for 2% -> 0% of each run, Pallas kernels for 0% -> 0%
where the time goes in v1:
time: 85.1 us; the launch traced here: 85 us
  Pallas kernels  81.2 us (95%)
  local copies, waits for them, and re-layouts  3.11 us (4%)
    pallas_call x1, Pallas kernels, local(): pl.pallas_call(functools.partial(kernel, sizes), out_shape=(shape, shape)...  81.2 us
    unnamed x6, local copies, waits for them, and re-layouts  3.11 us

profile of v1, /device:TPU:1, one launch (start us, length us, event | category | flops | bytes accessed | tf_op | source)
XLA Modules:
  0.0 85.0 jit_solution(3660440335243121028)
XLA Ops:
  0.6 0.0 copy-start
  0.6 0.9 %copy-done = f32[16,16,128]{2,1,0:T(8,128)S(1)} copy-done((f32[16,16,128]{2,1,0:T(8,128)S(1)}, f32[16,16,128]{2,1,0:T(8,128)}, u32[]{:S(2)}) %copy-start) | copy-done | bytes 131096
  1.5 0.0 copy-start.1
  1.5 0.9 %copy-done.1 = f32[16,16,128]{2,1,0:T(8,128)S(1)} copy-done((f32[16,16,128]{2,1,0:T(8,128)S(1)}, f32[16,16,128]{2,1,0:T(8,128)}, u32[]{:S(2)}) %copy-start.1) | copy-done | bytes 131096
  2.4 81.2 %heat_sink_step.1 = (f32[16,16,128]{2,1,0:T(8,128)S(1)}, f32[16,16,128]{2,1,0:T(8,128)S(1)}) custom-call(f32[16,16,128]{2,1,0:T(8,128)S(1)} %copy-done, f32[16,16,128]{2,1,0:T(8,128)S(1)} %copy-done.1), custom_call_target="tpu_custom_call" | custom-call | tf_op jit(solution)/shard_map/heat_sink_step/pallas_call | solution.py:637
  83.7 0.7 copy.6
  84.3 0.7 copy.7
Async XLA Ops:
  0.6 0.9 %copy-start = (f32[16,16,128]{2,1,0:T(8,128)S(1)}, f32[16,16,128]{2,1,0:T(8,128)}, u32[]{:S(2)}) copy-start(f32[16,16,128]{2,1,0:T(8,128)} %rho_ref.1) | copy-start | bytes 393220
  1.5 0.9 %copy-start.1 = (f32[16,16,128]{2,1,0:T(8,128)S(1)}, f32[16,16,128]{2,1,0:T(8,128)}, u32[]{:S(2)}) copy-start(f32[16,16,128]{2,1,0:T(8,128)} %src_ref.1) | copy-start | bytes 393220

commit v2 on v1

--- a/solution.py
+++ b/solution.py
@@ -65,7 +65,8 @@
 
 
 def loop(lower, upper, body):
-    lax.fori_loop(lower, upper, lambda i, c: (body(i), c)[1], 0)
+    for i in range(lower, upper):
+        body(i)
 
 
 class Exchange:
@@ -452,7 +453,9 @@
         return tuple(a + t[0:8] + t[8:16] for a, t in zip(acc, terms))
 
     zero = jnp.zeros((8, LANES), F32)
-    acc = lax.fori_loop(PAD, PAD + NZ, dots, (zero,) * 6)
+    acc = (zero,) * 6
+    for z in range(PAD, PAD + NZ):
+        acc = dots(z, acc)
     which = lax.broadcasted_iota(jnp.int32, (8, LANES), 0)
     part = zero
     for i, a in enumerate(acc):

time: 85.1 us -> 60.8 us (0.71)
  Pallas kernels: 81.2 us -> 56.9 us
    pallas_call x1, Pallas kernels: 81.2 us -> 56.9 us  [local(): pl.pallas_call(functools.partial(kernel, sizes), out_shape=(shape, shape)...]
where the time goes in v2:
time: 60.8 us; the launch traced here: 60.7 us
  Pallas kernels  56.9 us (94%)
  local copies, waits for them, and re-layouts  3.11 us (5%)
  between operations  0.65 us (1%)
    pallas_call x1, Pallas kernels, local(): pl.pallas_call(functools.partial(kernel, sizes), out_shape=(shape, shape)...  56.9 us
    unnamed x6, local copies, waits for them, and re-layouts  3.11 us

profile of v2, /device:TPU:1, one launch (start us, length us, event | category | flops | bytes accessed | tf_op | source)
XLA Modules:
  0.0 60.7 jit_solution(2626992216103010452)
XLA Ops:
  0.6 0.0 copy-start
  0.6 0.9 %copy-done = f32[16,16,128]{2,1,0:T(8,128)S(1)} copy-done((f32[16,16,128]{2,1,0:T(8,128)S(1)}, f32[16,16,128]{2,1,0:T(8,128)}, u32[]{:S(2)}) %copy-start) | copy-done | bytes 131096
  1.5 0.0 copy-start.1
  1.5 0.9 %copy-done.1 = f32[16,16,128]{2,1,0:T(8,128)S(1)} copy-done((f32[16,16,128]{2,1,0:T(8,128)S(1)}, f32[16,16,128]{2,1,0:T(8,128)}, u32[]{:S(2)}) %copy-start.1) | copy-done | bytes 131096
  2.4 56.9 %heat_sink_step.1 = (f32[16,16,128]{2,1,0:T(8,128)S(1)}, f32[16,16,128]{2,1,0:T(8,128)S(1)}) custom-call(f32[16,16,128]{2,1,0:T(8,128)S(1)} %copy-done, f32[16,16,128]{2,1,0:T(8,128)S(1)} %copy-done.1), custom_call_target="tpu_custom_call" | custom-call | tf_op jit(solution)/shard_map/heat_sink_step/pallas_call | solution.py:640
  59.4 0.7 %copy.6 = f32[16,16,128]{2,1,0:T(8,128)} copy(f32[16,16,128]{2,1,0:T(8,128)S(1)} %get-tuple-element.4) | data formatting | bytes 262144
  60.0 0.7 %copy.7 = f32[16,16,128]{2,1,0:T(8,128)} copy(f32[16,16,128]{2,1,0:T(8,128)S(1)} %get-tuple-element.5) | data formatting | bytes 262144
Async XLA Ops:
  0.6 0.9 %copy-start = (f32[16,16,128]{2,1,0:T(8,128)S(1)}, f32[16,16,128]{2,1,0:T(8,128)}, u32[]{:S(2)}) copy-start(f32[16,16,128]{2,1,0:T(8,128)} %rho_ref.1) | copy-start | bytes 393220
  1.5 0.9 %copy-start.1 = (f32[16,16,128]{2,1,0:T(8,128)S(1)}, f32[16,16,128]{2,1,0:T(8,128)}, u32[]{:S(2)}) copy-start(f32[16,16,128]{2,1,0:T(8,128)} %src_ref.1) | copy-start | bytes 393220

commit v3 on v2

--- a/solution.py
+++ b/solution.py
@@ -60,7 +60,7 @@
 
 
 def pair_lanes(v):
-    even = lax.rem(lane_iota(v.shape[0]), 2) == 0
+    even = (lane_iota(v.shape[0]) & 1) == 0
     return v + jnp.where(even, pltpu.roll(v, LANES - 1, 1), pltpu.roll(v, 1, 1))
 
 
@@ -70,41 +70,46 @@
 
 
 class Exchange:
-    def __init__(self, sizes, arr, fields, halo, n, group, pks, pkr, ssem, rsem):
-        self.sizes, self.arr, self.fields, self.halo, self.n = sizes, arr, fields, halo, n
-        self.group = group
+    def __init__(self, sizes, arr, depth, rows, group, pks, pkr, ssem, rsem):
+        self.sizes, self.arr, self.depth, self.rows, self.group = sizes, arr, depth, rows, group
+        self.fields = arr.shape[0]
         self.per = LANES // group
         self.pks, self.pkr, self.ssem, self.rsem = pks, pkr, ssem, rsem
         self.copies = []
 
+    def slot(self, plane, f):
+        return divmod(plane * self.fields + f, self.per)
+
     def pack(self):
-        per, group, n = self.per, self.group, self.n
-        lane = lane_iota(n)
-        for f in range(self.fields):
-            for g in range(n // per):
-                acc = None
-                for k in range(per):
-                    v = self.arr[f, 0, PAD + g * per + k, PAD : PAD + n, :]
-                    v = pltpu.roll(v, group * k + group // 2, 1)
-                    acc = v if acc is None else jnp.where(lane >= group * k, v, acc)
-                self.pks[f, g] = acc
+        (nz, pz, _), (nr, pr, _) = self.depth, self.rows
+        slot_of = lane_iota(nr) >> (self.group.bit_length() - 1)
+        packed = {}
+        for p in range(nz):
+            for f in range(self.fields):
+                g, q = self.slot(p, f)
+                v = self.arr[f, 0, pz + p, pr : pr + nr, :]
+                v = pltpu.roll(v, self.group * q, 1) if q else v
+                for side, at in ((0, q), (1, (q + self.per - 1) % self.per)):
+                    old = packed.get((side, g))
+                    packed[side, g] = v if old is None else jnp.where(slot_of == at, v, old)
+        for (side, g), v in packed.items():
+            self.pks[side, g] = v
 
     def start(self):
-        n, h, per = self.n, self.halo, self.per
-        groups = n // per
-        side_groups = -(-h // per)
+        (nz, pz, hz), (nr, pr, hr) = self.depth, self.rows
+        groups = self.slot(nz - 1, self.fields - 1)[0] + 1
         for i, (dz, dx, dy) in enumerate(NEIGHBOURS):
-            rows = {0: (0, n, PAD), 1: (n - PAD, PAD, 0), -1: (0, PAD, PAD + n)}[dx]
+            r = {0: (0, nr, pr), 1: (nr - hr, hr, pr - hr), -1: (0, hr, pr + nr)}[dx]
             if dy == 0:
-                planes = {0: (0, n, PAD), 1: (n - h, h, PAD - h), -1: (0, h, PAD + n)}[dz]
-                src = self.arr.at[:, 0, pl.ds(PAD + planes[0], planes[1]), pl.ds(PAD + rows[0], rows[1]), :]
-                dst = self.arr.at[:, 0, pl.ds(planes[2], planes[1]), pl.ds(rows[2], rows[1]), :]
+                z = {0: (0, nz, pz), 1: (nz - hz, hz, pz - hz), -1: (0, hz, pz + nz)}[dz]
+                src = self.arr.at[:, 0, pl.ds(pz + z[0], z[1]), pl.ds(pr + r[0], r[1]), :]
+                dst = self.arr.at[:, 0, pl.ds(z[2], z[1]), pl.ds(r[2], r[1]), :]
             else:
-                first = PAD // per
-                s = side_groups
-                gr = {0: (0, groups, first), 1: (groups - s, s, first - s), -1: (0, s, first + groups)}[dz]
-                src = self.pks.at[:, pl.ds(gr[0], gr[1]), pl.ds(rows[0], rows[1]), :]
-                dst = self.pkr.at[0 if dy == 1 else 1, :, pl.ds(gr[2], gr[1]), pl.ds(rows[2], rows[1]), :]
+                first = self.slot(nz - hz, 0)[0] if dz == 1 else 0
+                end = self.slot(hz - 1, self.fields - 1)[0] + 1 if dz == -1 else groups
+                g = pl.ds(first, end - first)
+                src = self.pks.at[0 if dy == -1 else 1, g, pl.ds(r[0], r[1]), :]
+                dst = self.pkr.at[0 if dy == -1 else 1, 1 - dz, g, pl.ds(r[2], r[1]), :]
             cp = pltpu.make_async_remote_copy(
                 src_ref=src,
                 dst_ref=dst,
@@ -121,21 +126,16 @@
             cp.wait_recv()
 
     def unpack(self):
-        per, group, n, h = self.per, self.group, self.n, self.halo
-        rows = n + 2 * PAD
-        low = lax.rem(lane_iota(rows), group) < group // 2
-
-        def body(g):
-            for f in range(self.fields):
-                merged = jnp.where(low, self.pkr[0, f, g], self.pkr[1, f, g])
-                for k in range(per):
-                    self.arr[f, 1, g * per + k, 0:rows, :] = pltpu.roll(
-                        merged, LANES - group * k - group // 2, 1
-                    )
-
-        first = (PAD - h) // per
-        last = -(-(PAD + n + h) // per)
-        loop(first, last, body)
+        (nz, pz, hz), (nr, pr, hr) = self.depth, self.rows
+        rows = nr + 2 * pr
+        slot_of = lane_iota(rows) >> (self.group.bit_length() - 1)
+        for region, planes in ((0, range(nz - hz, nz)), (1, range(nz)), (2, range(hz))):
+            for p in planes:
+                for f in range(self.fields):
+                    g, q = self.slot(p, f)
+                    v = jnp.where(slot_of == q, self.pkr[0, region, g], self.pkr[1, region, g])
+                    v = pltpu.roll(v, LANES - self.group * q, 1) if q else v
+                    self.arr[f, 1, pz + (region - 1) * nz + p, 0:rows, :] = v
 
     def finish(self):
         for cp in self.copies:
@@ -160,11 +160,13 @@
     vv,
     z0,
     q0,
-    last,
+    lz,
+    lw,
     ww,
     mask,
     cin,
     cin2,
+    rhs,
     cc,
     kcz,
     kcx,
@@ -184,10 +186,16 @@
     pkr3,
     pks4,
     pkr4,
+    pks5,
+    pkr5,
+    red0,
     red1,
     red2,
+    insem,
     ssems,
     rsems,
+    rs0,
+    rr0,
     rs1,
     rr1,
     rs2,
@@ -196,26 +204,28 @@
     gxs, gys, gzs = sizes
     gx, gy, gz = lax.axis_index("gx"), lax.axis_index("gy"), lax.axis_index("gz")
 
-    def peer1(dy, dz):
-        return (gx, lax.rem(gy + dy, gys), lax.rem(gz + 2 * dz, gzs))
-
-    def peer2(dx, flip):
-        return (lax.rem(gx + dx, gxs), gy, other_core() if flip else gz)
+    def peer0(_):
+        return (gx, gy, other_core())
+
+    def peer1(o):
+        return (gx, lax.rem(gy + o[0], gys), lax.rem(gz + 2 * o[1], gzs))
+
+    def peer2(dx):
+        return (lax.rem(gx + dx, gxs), gy, gz)
 
     group1 = [(dy, dz) for dy in range(gys) for dz in range(gzs // 2) if (dy, dz) != (0, 0)]
-    group2 = [(dx, fl) for dx in range(gxs) for fl in range(2) if (dx, fl) != (0, 0)]
-
+    group2 = list(range(1, gxs))
+
+    loads = [
+        pltpu.make_async_copy(ref, fin.at[f, 0, pl.ds(PAD, NZ), pl.ds(PAD, NX), :], insem.at[f])
+        for f, ref in enumerate((rho_ref, src_ref))
+    ]
+    for cp in loads:
+        cp.start()
     barrier = pltpu.get_barrier_semaphore()
     partners = [place(sizes, o) for o in NEIGHBOURS]
-    partners += [peer1(*o) for o in group1 if o not in ((1, 0), (gys - 1, 0))]
-    partners += [peer2(*o) for o in group2 if o[0] not in (0, 1, gxs - 1)]
     for device in partners:
         pl.semaphore_signal(barrier, inc=1, device_id=device, device_id_type=MESH)
-
-    fin[0, 0, PAD : PAD + NZ, PAD : PAD + NX, :] = rho_ref[...]
-    fin[1, 0, PAD : PAD + NZ, PAD : PAD + NX, :] = src_ref[...]
-    ex1 = Exchange(sizes, fin, 2, 5, NZ, 16, pks1, pkr1, ssems.at[0], rsems.at[0])
-    ex1.pack()
 
     row = lax.broadcasted_iota(jnp.int32, (FZ, LANES), 0) - PAD + gx * NX
     lane = lane_iota(FZ)
@@ -226,8 +236,8 @@
     side_in = row_in & ((lane < right_end) | (lane >= left_start))
     mask[0] = jnp.where(row_in, 1.0, 0.0)
     mask[1] = jnp.where(side_in, 1.0, 0.0)
-    crow = lax.broadcasted_iota(jnp.int32, (24, LANES), 0) - PAD + gx * CX
-    clane = lane_iota(24)
+    crow = lax.broadcasted_iota(jnp.int32, (32, LANES), 0) - PAD + gx * CX
+    clane = lane_iota(32)
     crow_in = (crow >= 0) & (crow < gxs * CX)
     cside_in = crow_in & (
         (clane < jnp.where(right, 16, 0)) | (clane >= jnp.where(left, LANES - 16, LANES))
@@ -239,6 +249,10 @@
         g = gz * cells + z - PAD
         return jnp.where((g >= 0) & (g < gzs * cells), 1.0, 0.0).astype(F32)
 
+    ex1 = Exchange(sizes, fin, (NZ, PAD, 5), (NX, PAD, 5), 8, pks1, pkr1, ssems.at[0], rsems.at[0])
+    for cp in loads:
+        cp.wait()
+    ex1.pack()
     pl.semaphore_wait(barrier, len(partners))
     ex1.start()
     ex1.wait()
@@ -291,76 +305,74 @@
             out.append((t + u) + v)
         return out
 
-    def coarse_rhs(load, field, dest):
-        def body(k):
-            total = None
-            for j in range(2):
-                z = PAD + 2 * k + j
-                t = (1.0 - OMEGA) * load(z) + off_diagonal(field, z, PAD, NX, 1)[0]
-                total = t if total is None else total + t
-            tmp[k, 0, 0:NX, :] = pair_lanes(total)
-            dest[0, 0, PAD + k, PAD : PAD + CX, :] = (
-                tmp[k, 0, pl.ds(0, CX, 2), :] + tmp[k, 0, pl.ds(1, CX, 2), :]
-            )
-
-        loop(0, CZ, body)
-
-    coarse_rhs(lambda z: fin[1, 0, z, PAD : PAD + NX, :], zpre, cin)
-
-    def coarse_cond(vc):
-        z = 2 * vc - PAD
-        for s in range(2):
-            u = cond[s, z, 0:FZ, :] + cond[s, z + 1, 0:FZ, :]
-            refined[vc, s] = pair_lanes(u)
-            cc[s, vc, 4:20, :] = 0.125 * (
-                refined[vc, s, pl.ds(0, 16, 2), :] + refined[vc, s, pl.ds(1, 16, 2), :]
-            )
-
-    loop(7, 17, coarse_cond)
-
-    def coarse_diag(vc):
-        c = cc[0, vc, 8:16, :]
-        ahead, behind = lane_neighbours(c, cc[1, vc, 8:16, :], 2)
-        t = cc[0, vc - 1, 8:16, :] + cc[0, vc + 1, 8:16, :]
-        t = t + (cc[0, vc, 7:15, :] + cc[0, vc, 9:17, :])
-        t = t + (ahead[0] + behind[0])
-        cin[1, 0, vc, 8:16, :] = c
-        cin[2, 0, vc, 8:16, :] = OMEGA / (2.0 * (6.0 * c + t))
-
-    loop(8, 16, coarse_diag)
-
-    ex2 = Exchange(sizes, cin, 3, 5, CZ, 32, pks2, pkr2, ssems.at[1], rsems.at[1])
+    even8 = (lane_iota(CX) & 1) == 0
+    even24 = (lane_iota(24) & 1) == 0
+
+    def block_rows(total, k):
+        tmp[k] = pair_lanes(total)
+        return tmp[k, pl.ds(0, CX, 2), :] + tmp[k, pl.ds(1, CX, 2), :]
+
+    def coarse_rhs(load, field, k):
+        total = None
+        for j in range(2):
+            z = PAD + 2 * k + j
+            t = (1.0 - OMEGA) * load(z) + off_diagonal(field, z, PAD, NX, 1)[0]
+            total = t if total is None else total + t
+        return block_rows(total, k)
+
+    for k in range(CZ):
+        z = PAD + 2 * k
+        c = cond[0, z, PAD : PAD + NX, :] + cond[0, z + 1, PAD : PAD + NX, :]
+        c = 0.125 * block_rows(c, CZ + k)
+        r = coarse_rhs(lambda z: fin[1, 0, z, PAD : PAD + NX, :], zpre, k)
+        cin[0, 0, PAD + k, PAD : PAD + CX, :] = jnp.where(even8, c, r)
+
+    ex2 = Exchange(sizes, cin, (CZ, PAD, 6), (CX, PAD, 6), 16, pks2, pkr2, ssems.at[1], rsems.at[1])
     ex2.pack()
     ex2.start()
     ex2.wait()
     ex2.unpack()
 
+    def split(v):
+        return (
+            jnp.where(even24, v, pltpu.roll(v, 1, 1)),
+            jnp.where(even24, pltpu.roll(v, LANES - 1, 1), v),
+        )
+
     def coarse_masked(vc):
         inside = plane_in(vc, CZ)
         for s in range(2):
-            ok = cmask[s] * inside > 0.5
-            cc[s, vc, 0:24, :] = jnp.where(ok, cin[1, s, vc, 0:24, :], 0.0)
-            i = jnp.where(ok, cin[2, s, vc, 0:24, :], 0.0)
-            cinv[s, vc, 0:24, :] = i
-            ea[s, vc, 0:24, :] = i * cin[0, s, vc, 0:24, :]
-
-    loop(3, 21, coarse_masked)
+            c, r = split(cin[0, s, vc, 0:24, :])
+            cc[s, vc, 0:24, :] = jnp.where(cmask[s, 0:24, :] * inside > 0.5, c, 0.0)
+            rhs[s, vc, 0:24, :] = r
+
+    loop(2, 22, coarse_masked)
 
     def coarse_faces(vc):
-        lo, hi = CLO, CLO + CWIN
+        lo, hi = 3, 27
         here = [cc[s, vc, lo:hi, :] for s in range(2)]
         ahead, behind = lane_neighbours(here[0], here[1], 2)
+        inside = plane_in(vc, CZ)
         for s in range(2):
             c = here[s]
-            kcz[s, vc, lo:hi, :] = 2.0 * (c + cc[s, vc - 1, lo:hi, :])
-            kcx[s, vc, lo:hi, :] = 2.0 * (c + cc[s, vc, lo + 1 : hi + 1, :])
-            kcx[s, vc, lo - 1 : lo, :] = 2.0 * (c[0:1, :] + cc[s, vc, lo - 1 : lo, :])
-            kcyp[s, vc, lo:hi, :] = 2.0 * (c + ahead[s])
-            kcym[s, vc, lo:hi, :] = 2.0 * (c + behind[s])
-
-    loop(4, 21, coarse_faces)
-
-    def sweep(e, e_next, rhs, first, end):
+            zm = 2.0 * (c + cc[s, vc - 1, lo:hi, :])
+            zp = 2.0 * (c + cc[s, vc + 1, lo:hi, :])
+            xm = 2.0 * (c + cc[s, vc, lo - 1 : hi - 1, :])
+            xp = 2.0 * (c + cc[s, vc, lo + 1 : hi + 1, :])
+            yp = 2.0 * (c + ahead[s])
+            ym = 2.0 * (c + behind[s])
+            kcz[s, vc, lo:hi, :] = zm
+            kcx[s, vc, lo:hi, :] = xp
+            kcyp[s, vc, lo:hi, :] = yp
+            kcym[s, vc, lo:hi, :] = ym
+            d = (zm + zp) + (xm + xp) + (yp + ym)
+            i = jnp.where(cmask[s, lo:hi, :] * inside > 0.5, OMEGA / d, 0.0)
+            cinv[s, vc, lo:hi, :] = i
+            ea[s, vc, lo:hi, :] = i * rhs[s, vc, lo:hi, :]
+
+    loop(3, 21, coarse_faces)
+
+    def sweep(e, e_next, first, end):
         lo, hi = CLO, CLO + CWIN
 
         def body(vc):
@@ -372,7 +384,7 @@
                 u = kcx[s, vc, lo:hi, :] * e[s, vc, lo + 1 : hi + 1, :]
                 u = u + kcx[s, vc, lo - 1 : hi - 1, :] * e[s, vc, lo - 1 : hi - 1, :]
                 v = kcyp[s, vc, lo:hi, :] * ahead[s] + kcym[s, vc, lo:hi, :] * behind[s]
-                r = rhs[0, s, vc, lo:hi, :] + ((t + u) + v)
+                r = rhs[s, vc, lo:hi, :] + ((t + u) + v)
                 e_next[s, vc, lo:hi, :] = (1.0 - OMEGA) * here[s] + cinv[s, vc, lo:hi, :] * r
 
         loop(first, end, body)
@@ -390,9 +402,9 @@
 
         loop(first, end, body)
 
-    sweep(ea, eb, cin, 4, 20)
-    sweep(eb, ea, cin, 5, 19)
-    sweep(ea, eb, cin, 6, 18)
+    sweep(ea, eb, 4, 20)
+    sweep(eb, ea, 5, 19)
+    sweep(ea, eb, 6, 18)
     add_refined(eb, zpre, 6, 18)
 
     def post(z):
@@ -413,21 +425,37 @@
 
     loop(6, 26, image)
 
-    coarse_rhs(lambda z: q0[0, z, PAD : PAD + NX, :], zpre, cin2)
-    ex3 = Exchange(sizes, cin2, 1, 4, CZ, 32, pks3, pkr3, ssems.at[2], rsems.at[2])
+    for k in range(CZ // 2):
+        r = [
+            coarse_rhs(lambda z: q0[0, z, PAD : PAD + NX, :], zpre, 2 * k + j) for j in range(2)
+        ]
+        cin2[0, 0, PAD // 2 + k, PAD : PAD + CX, :] = jnp.where(even8, r[0], r[1])
+    ex3 = Exchange(
+        sizes, cin2, (CZ // 2, PAD // 2, 2), (CX, PAD, 4), 8, pks3, pkr3, ssems.at[2], rsems.at[2]
+    )
     ex3.pack()
     ex3.start()
+
+    own = slice(PAD, PAD + NX)
+    for z in range(PAD, PAD + NZ):
+        lz[0, 0, z, own, :] = z0[0, z, own, :]
+    ex4 = Exchange(sizes, lz, (NZ, PAD, 4), (NX, PAD, 4), 8, pks4, pkr4, ssems.at[3], rsems.at[3])
+    ex4.pack()
     ex3.wait()
+    ex4.start()
     ex3.unpack()
 
-    def first_correction(vc):
-        for s in range(2):
-            ea[s, vc, 0:24, :] = cinv[s, vc, 0:24, :] * cin2[0, s, vc, 0:24, :]
-
-    loop(4, 20, first_correction)
-    sweep(ea, eb, cin2, 5, 19)
-    sweep(eb, ea, cin2, 6, 18)
-    sweep(ea, eb, cin2, 7, 17)
+    def first_correction(v2):
+        for s in range(2):
+            for j, r in enumerate(split(cin2[0, s, v2, 0:24, :])):
+                vc = 2 * v2 + j
+                rhs[s, vc, 0:24, :] = r
+                ea[s, vc, 3:27, :] = cinv[s, vc, 3:27, :] * rhs[s, vc, 3:27, :]
+
+    loop(2, 10, first_correction)
+    sweep(ea, eb, 5, 19)
+    sweep(eb, ea, 6, 18)
+    sweep(ea, eb, 7, 17)
     add_refined(eb, zpre, 7, 17)
 
     def post_second(z):
@@ -438,8 +466,6 @@
             )
 
     loop(7, 25, post_second)
-
-    own = slice(PAD, PAD + NX)
 
     def dots(z, acc):
         w = ww[0, z, own, :]
@@ -447,8 +473,7 @@
         q = q0[0, z, own, :]
         r = fin[1, 0, z, own, :]
         p = diag[0, z, own, :] * w - off_diagonal(ww, z, PAD, NX, 1)[0]
-        last[0, 0, z, own, :] = zz
-        last[1, 0, z, own, :] = w
+        lw[0, 0, z, own, :] = w
         terms = (r * zz, zz * q, r * w, q * w, zz * p, w * p)
         return tuple(a + t[0:8] + t[8:16] for a, t in zip(acc, terms))
 
@@ -461,49 +486,46 @@
     for i, a in enumerate(acc):
         part = jnp.where(which == i, jnp.sum(a, axis=0, keepdims=True), part)
 
-    rank1 = gy * (gzs // 2) + gz // 2
-    red1[rank1] = part
-    cps1 = []
-    for i, o in enumerate(group1):
-        cp = pltpu.make_async_remote_copy(
-            src_ref=red1.at[rank1],
-            dst_ref=red1.at[rank1],
-            send_sem=rs1.at[i],
-            recv_sem=rr1.at[i],
-            device_id=peer1(*o),
-            device_id_type=MESH,
-        )
-        cp.start()
-        cps1.append(cp)
-    ex4 = Exchange(sizes, last, 2, 4, NZ, 16, pks4, pkr4, ssems.at[3], rsems.at[3])
-    ex4.pack()
-    ex4.start()
-    for cp in cps1:
-        cp.wait_recv()
-    part = red1[0]
-    for i in range(1, len(group1) + 1):
-        part = part + red1[i]
-    rank2 = gx * 2 + lax.rem(gz, 2)
-    red2[rank2] = part
-    cps2 = []
-    for i, o in enumerate(group2):
-        cp = pltpu.make_async_remote_copy(
-            src_ref=red2.at[rank2],
-            dst_ref=red2.at[rank2],
-            send_sem=rs2.at[i],
-            recv_sem=rr2.at[i],
-            device_id=peer2(*o),
-            device_id_type=MESH,
-        )
-        cp.start()
-        cps2.append(cp)
+    reduce_copies = []
+
+    def share(part, slots, rank, offsets, peer, ssem, rsem):
+        slots[rank] = part
+        copies = []
+        for i, o in enumerate(offsets):
+            cp = pltpu.make_async_remote_copy(
+                src_ref=slots.at[rank],
+                dst_ref=slots.at[rank],
+                send_sem=ssem.at[i],
+                recv_sem=rsem.at[i],
+                device_id=peer(o),
+                device_id_type=MESH,
+            )
+            cp.start()
+            copies.append(cp)
+        reduce_copies.extend(copies)
+        return copies
+
+    def total_of(slots, copies):
+        for cp in copies:
+            cp.wait_recv()
+        values = [slots[i] for i in range(slots.shape[0])]
+        while len(values) > 1:
+            values = [a + b for a, b in zip(values[0::2], values[1::2])]
+        return values[0]
+
+    copies = share(part, red0, lax.rem(gz, 2), [0], peer0, rs0, rr0)
+    ex5 = Exchange(sizes, lw, (NZ, PAD, 4), (NX, PAD, 4), 8, pks5, pkr5, ssems.at[4], rsems.at[4])
+    ex5.pack()
+    part = total_of(red0, copies)
+    copies = share(part, red1, gy * (gzs // 2) + gz // 2, group1, peer1, rs1, rr1)
+    ex5.start()
     ex4.wait()
     ex4.unpack()
-    for cp in cps2:
-        cp.wait_recv()
-    total = red2[0]
-    for i in range(1, len(group2) + 1):
-        total = total + red2[i]
+    part = total_of(red1, copies)
+    copies = share(part, red2, gx, group2, peer2, rs2, rr2)
+    ex5.wait()
+    ex5.unpack()
+    total = total_of(red2, copies)
     total = jnp.broadcast_to(jnp.sum(total, axis=1, keepdims=True), (8, LANES))
     rz, zq, rw, qw, zp, wp = (total[i : i + 1, :] for i in range(6))
     a0 = rz / zq
@@ -517,7 +539,7 @@
     def solution_plane(z):
         inside = plane_in(z, NZ)
         for s in range(2):
-            x = c1 * last[0, s, z, LO:HI, :] + c2 * last[1, s, z, LO:HI, :]
+            x = c1 * lz[0, s, z, LO:HI, :] + c2 * lw[0, s, z, LO:HI, :]
             vv[s, z, LO:HI, :] = x * (mask[s, LO:HI, :] * inside)
 
     loop(4, 28, solution_plane)
@@ -588,14 +610,14 @@
 
     loop(0, NZ, blur_out)
 
-    for ex in (ex1, ex2, ex3, ex4):
+    for ex in (ex1, ex2, ex3, ex4, ex5):
         ex.finish()
-    for cp in cps1 + cps2:
+    for cp in reduce_copies:
         cp.wait_send()
 
 
 def local(sizes, density, volume_power_source):
-    shape = jax.ShapeDtypeStruct((NZ, NX, LANES), F32)
+    shape = pltpu.VMEM((NZ, NX, LANES), F32)
     vmem = pl.BlockSpec(memory_space=pltpu.VMEM)
 
     def fine(*lead, rows=FZ):
@@ -604,50 +626,48 @@
     def coarse(*lead):
         return pltpu.VMEM((*lead, 2, CZP, 32, LANES), F32)
 
+    def packs(groups, rows):
+        own = pltpu.VMEM((2, groups, rows, LANES), F32)
+        return own, pltpu.VMEM((2, 3, groups, rows + 2 * PAD, LANES), F32)
+
     n = len(NEIGHBOURS)
-    g1 = sizes[1] * (sizes[2] // 2)
-    g2 = sizes[0] * 2
+    counts = (2, sizes[1] * (sizes[2] // 2), sizes[0])
     scratch = [
         fine(2),
         fine(rows=40),
         *[fine() for _ in range(10)],
-        fine(2),
+        fine(1),
+        fine(1),
         fine(),
         pltpu.VMEM((2, FZ, LANES), F32),
-        coarse(3),
         coarse(1),
-        *[coarse() for _ in range(8)],
-        pltpu.VMEM((2, 24, LANES), F32),
+        pltpu.VMEM((1, 2, CZP // 2, 32, LANES), F32),
+        *[coarse() for _ in range(9)],
+        pltpu.VMEM((2, 32, LANES), F32),
         pltpu.VMEM((CZP, 2, FZ, LANES), F32),
-        pltpu.VMEM((CZ, 1, NX, LANES), F32),
-        pltpu.VMEM((2, 2, NX, LANES), F32),
-        pltpu.VMEM((2, 2, 4, FZ, LANES), F32),
-        pltpu.VMEM((3, 2, CX, LANES), F32),
-        pltpu.VMEM((2, 3, 6, 24, LANES), F32),
-        pltpu.VMEM((1, 2, CX, LANES), F32),
-        pltpu.VMEM((2, 1, 6, 24, LANES), F32),
-        pltpu.VMEM((2, 2, NX, LANES), F32),
-        pltpu.VMEM((2, 2, 4, FZ, LANES), F32),
-        pltpu.VMEM((g1, 8, LANES), F32),
-        pltpu.VMEM((g2, 8, LANES), F32),
-        pltpu.SemaphoreType.DMA((4, n)),
-        pltpu.SemaphoreType.DMA((4, n)),
-        pltpu.SemaphoreType.DMA((g1 - 1,)),
-        pltpu.SemaphoreType.DMA((g1 - 1,)),
-        pltpu.SemaphoreType.DMA((g2 - 1,)),
-        pltpu.SemaphoreType.DMA((g2 - 1,)),
+        pltpu.VMEM((2 * CZ, NX, LANES), F32),
+        *packs(2, NX),
+        *packs(1, CX),
+        *packs(1, CX),
+        *packs(1, NX),
+        *packs(1, NX),
+        *[pltpu.VMEM((c, 8, LANES), F32) for c in counts],
+        pltpu.SemaphoreType.DMA((2,)),
+        pltpu.SemaphoreType.DMA((5, n)),
+        pltpu.SemaphoreType.DMA((5, n)),
+        *[pltpu.SemaphoreType.DMA((c - 1,)) for c in counts for _ in range(2)],
     ]
     return pl.pallas_call(
         functools.partial(kernel, sizes),
         out_shape=(shape, shape),
-        in_specs=[vmem, vmem],
+        in_specs=[pl.BlockSpec(memory_space=pltpu.HBM)] * 2,
         out_specs=(vmem, vmem),
         scratch_shapes=scratch,
         compiler_params=pltpu.CompilerParams(
             collective_id=0, has_side_effects=True, vmem_limit_bytes=48 * 1024 * 1024
         ),
         name="heat_sink_step",
-    )(density, volume_power_source)
+    )(*(pltpu.with_memory_space_constraint(x, pltpu.HBM) for x in (density, volume_power_source)))
 
 
 def solution(mesh):

time: 60.8 us -> 48.4 us (0.80)
  Pallas kernels: 56.9 us -> 46.3 us
  local copies, waits for them, and re-layouts: 3.11 us -> 1.31 us
    pallas_call x1, Pallas kernels: 56.9 us -> 46.3 us  [local(): pl.pallas_call(functools.partial(kernel, sizes), out_shape=(shape, shape)...]
    unnamed x6 -> x2, local copies, waits for them, and re-layouts: 3.11 us -> 1.31 us
where the time goes in v3:
time: 48.4 us; the launch traced here: 48.3 us
  Pallas kernels  46.3 us (96%)
  local copies, waits for them, and re-layouts  1.31 us (3%)
  between operations  0.64 us (1%)
    pallas_call x1, Pallas kernels, local(): pl.pallas_call(functools.partial(kernel, sizes), out_shape=(shape, shape)...  46.3 us
    unnamed x2, local copies, waits for them, and re-layouts  1.31 us

profile of v3, /device:TPU:1, one launch (start us, length us, event | category | flops | bytes accessed | tf_op | source)
XLA Modules:
  0.0 48.3 jit_solution(7955183506773578441)
XLA Ops:
  0.6 46.3 %heat_sink_step.1 = (f32[16,16,128]{2,1,0:T(8,128)S(1)}, f32[16,16,128]{2,1,0:T(8,128)S(1)}) custom-call(f32[16,16,128]{2,1,0:T(8,128)} %rho_ref.1, f32[16,16,128]{2,1,0:T(8,128)} %src_ref.1), custom_call_target="tpu_custom_call" | custom-call | tf_op jit(solution)/shard_map/heat_sink_step/pallas_call | solution.py:660
  47.0 0.7 %copy.6 = f32[16,16,128]{2,1,0:T(8,128)} copy(f32[16,16,128]{2,1,0:T(8,128)S(1)} %get-tuple-element.2) | data formatting | bytes 262144
  47.6 0.7 %copy.7 = f32[16,16,128]{2,1,0:T(8,128)} copy(f32[16,16,128]{2,1,0:T(8,128)S(1)} %get-tuple-element.3) | data formatting | bytes 262144

commit v4 on v3

--- a/solution.py
+++ b/solution.py
@@ -69,13 +69,18 @@
         body(i)
 
 
+def wait_rows(span, rows, sem):
+    view = span.at[pl.ds(0, rows)]
+    pltpu.make_async_copy(view, view, sem).wait()
+
+
 class Exchange:
-    def __init__(self, sizes, arr, depth, rows, group, pks, pkr, ssem, rsem):
+    def __init__(self, sizes, arr, depth, rows, group, pks, pkr, ssem, rsem, span):
         self.sizes, self.arr, self.depth, self.rows, self.group = sizes, arr, depth, rows, group
         self.fields = arr.shape[0]
         self.per = LANES // group
-        self.pks, self.pkr, self.ssem, self.rsem = pks, pkr, ssem, rsem
-        self.copies = []
+        self.pks, self.pkr, self.ssem, self.rsem, self.span = pks, pkr, ssem, rsem, span
+        self.sent = 0
 
     def slot(self, plane, f):
         return divmod(plane * self.fields + f, self.per)
@@ -98,7 +103,7 @@
     def start(self):
         (nz, pz, hz), (nr, pr, hr) = self.depth, self.rows
         groups = self.slot(nz - 1, self.fields - 1)[0] + 1
-        for i, (dz, dx, dy) in enumerate(NEIGHBOURS):
+        for dz, dx, dy in NEIGHBOURS:
             r = {0: (0, nr, pr), 1: (nr - hr, hr, pr - hr), -1: (0, hr, pr + nr)}[dx]
             if dy == 0:
                 z = {0: (0, nz, pz), 1: (nz - hz, hz, pz - hz), -1: (0, hz, pz + nz)}[dz]
@@ -113,17 +118,19 @@
             cp = pltpu.make_async_remote_copy(
                 src_ref=src,
                 dst_ref=dst,
-                send_sem=self.ssem.at[i],
-                recv_sem=self.rsem.at[i],
+                send_sem=self.ssem,
+                recv_sem=self.rsem,
                 device_id=place(self.sizes, (dz, dx, dy)),
                 device_id_type=MESH,
             )
             cp.start()
-            self.copies.append(cp)
+            count = 1
+            for d in src.shape:
+                count *= d
+            self.sent += count // LANES
 
     def wait(self):
-        for cp in self.copies:
-            cp.wait_recv()
+        wait_rows(self.span, self.sent, self.rsem)
 
     def unpack(self):
         (nz, pz, hz), (nr, pr, hr) = self.depth, self.rows
@@ -138,8 +145,7 @@
                     self.arr[f, 1, pz + (region - 1) * nz + p, 0:rows, :] = v
 
     def finish(self):
-        for cp in self.copies:
-            cp.wait_send()
+        wait_rows(self.span, self.sent, self.ssem)
 
 
 def kernel(
@@ -191,15 +197,10 @@
     red0,
     red1,
     red2,
+    span,
     insem,
     ssems,
     rsems,
-    rs0,
-    rr0,
-    rs1,
-    rr1,
-    rs2,
-    rr2,
 ):
     gxs, gys, gzs = sizes
     gx, gy, gz = lax.axis_index("gx"), lax.axis_index("gy"), lax.axis_index("gz")
@@ -249,7 +250,7 @@
         g = gz * cells + z - PAD
         return jnp.where((g >= 0) & (g < gzs * cells), 1.0, 0.0).astype(F32)
 
-    ex1 = Exchange(sizes, fin, (NZ, PAD, 5), (NX, PAD, 5), 8, pks1, pkr1, ssems.at[0], rsems.at[0])
+    ex1 = Exchange(sizes, fin, (NZ, PAD, 5), (NX, PAD, 5), 8, pks1, pkr1, ssems.at[0], rsems.at[0], span)
     for cp in loads:
         cp.wait()
     ex1.pack()
@@ -327,7 +328,7 @@
         r = coarse_rhs(lambda z: fin[1, 0, z, PAD : PAD + NX, :], zpre, k)
         cin[0, 0, PAD + k, PAD : PAD + CX, :] = jnp.where(even8, c, r)
 
-    ex2 = Exchange(sizes, cin, (CZ, PAD, 6), (CX, PAD, 6), 16, pks2, pkr2, ssems.at[1], rsems.at[1])
+    ex2 = Exchange(sizes, cin, (CZ, PAD, 6), (CX, PAD, 6), 16, pks2, pkr2, ssems.at[1], rsems.at[1], span)
     ex2.pack()
     ex2.start()
     ex2.wait()
@@ -431,7 +432,7 @@
         ]
         cin2[0, 0, PAD // 2 + k, PAD : PAD + CX, :] = jnp.where(even8, r[0], r[1])
     ex3 = Exchange(
-        sizes, cin2, (CZ // 2, PAD // 2, 2), (CX, PAD, 4), 8, pks3, pkr3, ssems.at[2], rsems.at[2]
+        sizes, cin2, (CZ // 2, PAD // 2, 2), (CX, PAD, 4), 8, pks3, pkr3, ssems.at[2], rsems.at[2], span
     )
     ex3.pack()
     ex3.start()
@@ -439,7 +440,7 @@
     own = slice(PAD, PAD + NX)
     for z in range(PAD, PAD + NZ):
         lz[0, 0, z, own, :] = z0[0, z, own, :]
-    ex4 = Exchange(sizes, lz, (NZ, PAD, 4), (NX, PAD, 4), 8, pks4, pkr4, ssems.at[3], rsems.at[3])
+    ex4 = Exchange(sizes, lz, (NZ, PAD, 4), (NX, PAD, 4), 8, pks4, pkr4, ssems.at[3], rsems.at[3], span)
     ex4.pack()
     ex3.wait()
     ex4.start()
@@ -486,46 +487,42 @@
     for i, a in enumerate(acc):
         part = jnp.where(which == i, jnp.sum(a, axis=0, keepdims=True), part)
 
-    reduce_copies = []
-
-    def share(part, slots, rank, offsets, peer, ssem, rsem):
+    shared = []
+
+    def share(part, slots, rank, offsets, peer, sem):
         slots[rank] = part
-        copies = []
-        for i, o in enumerate(offsets):
-            cp = pltpu.make_async_remote_copy(
+        for o in offsets:
+            pltpu.make_async_remote_copy(
                 src_ref=slots.at[rank],
                 dst_ref=slots.at[rank],
-                send_sem=ssem.at[i],
-                recv_sem=rsem.at[i],
+                send_sem=ssems.at[sem],
+                recv_sem=rsems.at[sem],
                 device_id=peer(o),
                 device_id_type=MESH,
-            )
-            cp.start()
-            copies.append(cp)
-        reduce_copies.extend(copies)
-        return copies
-
-    def total_of(slots, copies):
-        for cp in copies:
-            cp.wait_recv()
+            ).start()
+        shared.append((8 * len(offsets), sem))
+
+    def total_of(slots):
+        rows, sem = shared[-1]
+        wait_rows(span, rows, rsems.at[sem])
         values = [slots[i] for i in range(slots.shape[0])]
         while len(values) > 1:
             values = [a + b for a, b in zip(values[0::2], values[1::2])]
         return values[0]
 
-    copies = share(part, red0, lax.rem(gz, 2), [0], peer0, rs0, rr0)
-    ex5 = Exchange(sizes, lw, (NZ, PAD, 4), (NX, PAD, 4), 8, pks5, pkr5, ssems.at[4], rsems.at[4])
+    share(part, red0, lax.rem(gz, 2), [0], peer0, 5)
+    ex5 = Exchange(sizes, lw, (NZ, PAD, 4), (NX, PAD, 4), 8, pks5, pkr5, ssems.at[4], rsems.at[4], span)
     ex5.pack()
-    part = total_of(red0, copies)
-    copies = share(part, red1, gy * (gzs // 2) + gz // 2, group1, peer1, rs1, rr1)
+    part = total_of(red0)
+    share(part, red1, gy * (gzs // 2) + gz // 2, group1, peer1, 6)
     ex5.start()
     ex4.wait()
     ex4.unpack()
-    part = total_of(red1, copies)
-    copies = share(part, red2, gx, group2, peer2, rs2, rr2)
+    part = total_of(red1)
+    share(part, red2, gx, group2, peer2, 7)
     ex5.wait()
     ex5.unpack()
-    total = total_of(red2, copies)
+    total = total_of(red2)
     total = jnp.broadcast_to(jnp.sum(total, axis=1, keepdims=True), (8, LANES))
     rz, zq, rw, qw, zp, wp = (total[i : i + 1, :] for i in range(6))
     a0 = rz / zq
@@ -612,8 +609,19 @@
 
     for ex in (ex1, ex2, ex3, ex4, ex5):
         ex.finish()
-    for cp in reduce_copies:
-        cp.wait_send()
+    for rows, sem in shared:
+        wait_rows(span, rows, ssems.at[sem])
+
+
+def store(t_ref, f_ref, out_t, out_f, sem):
+    copies = [
+        pltpu.make_async_copy(src, dst, sem.at[i])
+        for i, (src, dst) in enumerate(((t_ref, out_t), (f_ref, out_f)))
+    ]
+    for cp in copies:
+        cp.start()
+    for cp in copies:
+        cp.wait()
 
 
 def local(sizes, density, volume_power_source):
@@ -630,7 +638,6 @@
         own = pltpu.VMEM((2, groups, rows, LANES), F32)
         return own, pltpu.VMEM((2, 3, groups, rows + 2 * PAD, LANES), F32)
 
-    n = len(NEIGHBOURS)
     counts = (2, sizes[1] * (sizes[2] // 2), sizes[0])
     scratch = [
         fine(2),
@@ -652,12 +659,12 @@
         *packs(1, NX),
         *packs(1, NX),
         *[pltpu.VMEM((c, 8, LANES), F32) for c in counts],
+        pltpu.VMEM((2048, LANES), F32),
         pltpu.SemaphoreType.DMA((2,)),
-        pltpu.SemaphoreType.DMA((5, n)),
-        pltpu.SemaphoreType.DMA((5, n)),
-        *[pltpu.SemaphoreType.DMA((c - 1,)) for c in counts for _ in range(2)],
+        pltpu.SemaphoreType.DMA((8,)),
+        pltpu.SemaphoreType.DMA((8,)),
     ]
-    return pl.pallas_call(
+    outs = pl.pallas_call(
         functools.partial(kernel, sizes),
         out_shape=(shape, shape),
         in_specs=[pl.BlockSpec(memory_space=pltpu.HBM)] * 2,
@@ -668,6 +675,15 @@
         ),
         name="heat_sink_step",
     )(*(pltpu.with_memory_space_constraint(x, pltpu.HBM) for x in (density, volume_power_source)))
+    hbm = pl.BlockSpec(memory_space=pltpu.HBM)
+    return pl.pallas_call(
+        store,
+        out_shape=(jax.ShapeDtypeStruct((NZ, NX, LANES), F32),) * 2,
+        in_specs=[vmem, vmem],
+        out_specs=(hbm, hbm),
+        scratch_shapes=[pltpu.SemaphoreType.DMA((2,))],
+        name="store_outputs",
+    )(*(pltpu.with_memory_space_constraint(x, pltpu.VMEM) for x in outs))
 
 
 def solution(mesh):

time: 48.4 us -> 44.9 us (0.928)
  Pallas kernels: 46.3 us -> 44.1 us
  local copies, waits for them, and re-layouts: 1.31 us -> 0 us
    pallas_call x1, Pallas kernels: 46.3 us -> 43.4 us  [local(): pl.pallas_call(functools.partial(kernel, sizes), out_shape=(shape, shape)...]
    unnamed x2 -> x0, local copies, waits for them, and re-layouts: 1.31 us -> none
    pallas_call x0 -> x1, Pallas kernels: none -> 0.72 us  [local(): pl.pallas_call(store, out_shape=(jax.ShapeDtypeStruct((NZ, NX, LANES), F3...]
where the time goes in v4:
time: 44.9 us; the launch traced here: 44.8 us
  Pallas kernels  44.1 us (98%)
  between operations  0.64 us (1%)
    pallas_call x1, Pallas kernels, local(): pl.pallas_call(functools.partial(kernel, sizes), out_shape=(shape, shape)...  43.4 us

profile of v4, /device:TPU:1, one launch (start us, length us, event | category | flops | bytes accessed | tf_op | source)
XLA Modules:
  0.0 44.8 jit_solution(16968941452945731455)
XLA Ops:
  0.6 43.4 %heat_sink_step.1 = (f32[16,16,128]{2,1,0:T(8,128)S(1)}, f32[16,16,128]{2,1,0:T(8,128)S(1)}) custom-call(f32[16,16,128]{2,1,0:T(8,128)} %rho_ref.1, f32[16,16,128]{2,1,0:T(8,128)} %src_ref.1), custom_call_target="tpu_custom_call" | custom-call | tf_op jit(solution)/shard_map/heat_sink_step/pallas_call | solution.py:667
  44.0 0.7 %store_outputs.1 = (f32[16,16,128]{2,1,0:T(8,128)}, f32[16,16,128]{2,1,0:T(8,128)}) custom-call(f32[16,16,128]{2,1,0:T(8,128)S(1)} %get-tuple-element.4.t_ref, f32[16,16,128]{2,1,0:T(8,128)S(1)} %get-tuple-element.5.f_ref), custom_call_target="tpu_custom_call" | custom-call | tf_op jit(solution)/shard_map/store_outputs/pallas_call | solution.py:679

commit v5 on v4

--- a/solution.py
+++ b/solution.py
@@ -26,7 +26,7 @@
 
 NEIGHBOURS = sorted(
     (o for o in itertools.product((-1, 0, 1), repeat=3) if o != (0, 0, 0)),
-    key=lambda o: (sum(map(abs, o)), o),
+    key=lambda o: (-sum(map(abs, o)), o[2] == 0, o),
 )
 
 
@@ -132,12 +132,15 @@
     def wait(self):
         wait_rows(self.span, self.sent, self.rsem)
 
-    def unpack(self):
+    def unpack(self, near=0, far=PAD):
         (nz, pz, hz), (nr, pr, hr) = self.depth, self.rows
         rows = nr + 2 * pr
         slot_of = lane_iota(rows) >> (self.group.bit_length() - 1)
         for region, planes in ((0, range(nz - hz, nz)), (1, range(nz)), (2, range(hz))):
             for p in planes:
+                outside = {0: nz - p, 1: 0, 2: p + 1}[region]
+                if not near <= outside <= far:
+                    continue
                 for f in range(self.fields):
                     g, q = self.slot(p, f)
                     v = jnp.where(slot_of == q, self.pkr[0, region, g], self.pkr[1, region, g])
@@ -197,6 +200,7 @@
     red0,
     red1,
     red2,
+    parts,
     span,
     insem,
     ssems,
@@ -214,8 +218,12 @@
     def peer2(dx):
         return (lax.rem(gx + dx, gxs), gy, gz)
 
+    def hops(d, n):
+        return min(d, n - d)
+
     group1 = [(dy, dz) for dy in range(gys) for dz in range(gzs // 2) if (dy, dz) != (0, 0)]
-    group2 = list(range(1, gxs))
+    group1.sort(key=lambda o: -hops(o[0], gys) - hops(o[1], gzs // 2))
+    group2 = sorted(range(1, gxs), key=lambda o: -hops(o, gxs))
 
     loads = [
         pltpu.make_async_copy(ref, fin.at[f, 0, pl.ds(PAD, NZ), pl.ds(PAD, NX), :], insem.at[f])
@@ -227,6 +235,17 @@
     partners = [place(sizes, o) for o in NEIGHBOURS]
     for device in partners:
         pl.semaphore_signal(barrier, inc=1, device_id=device, device_id_type=MESH)
+
+    def plane_in(z, cells):
+        g = gz * cells + z - PAD
+        return jnp.where((g >= 0) & (g < gzs * cells), 1.0, 0.0).astype(F32)
+
+    ex1 = Exchange(sizes, fin, (NZ, PAD, 5), (NX, PAD, 5), 8, pks1, pkr1, ssems.at[0], rsems.at[0], span)
+    for cp in loads:
+        cp.wait()
+    ex1.pack()
+    pl.semaphore_wait(barrier, len(partners))
+    ex1.start()
 
     row = lax.broadcasted_iota(jnp.int32, (FZ, LANES), 0) - PAD + gx * NX
     lane = lane_iota(FZ)
@@ -246,18 +265,8 @@
     cmask[0] = jnp.where(crow_in, 1.0, 0.0)
     cmask[1] = jnp.where(cside_in, 1.0, 0.0)
 
-    def plane_in(z, cells):
-        g = gz * cells + z - PAD
-        return jnp.where((g >= 0) & (g < gzs * cells), 1.0, 0.0).astype(F32)
-
-    ex1 = Exchange(sizes, fin, (NZ, PAD, 5), (NX, PAD, 5), 8, pks1, pkr1, ssems.at[0], rsems.at[0], span)
-    for cp in loads:
-        cp.wait()
-    ex1.pack()
-    pl.semaphore_wait(barrier, len(partners))
-    ex1.start()
     ex1.wait()
-    ex1.unpack()
+    ex1.unpack(0, 2)
 
     def conductivity(z):
         inside = plane_in(z, NZ)
@@ -265,7 +274,7 @@
             r = fin[0, s, z]
             cond[s, z, 0:FZ, :] = (mask[s] * inside) * (KMIN + (1.0 - KMIN) * (r * r * r))
 
-    loop(3, 29, conductivity)
+    loop(6, 26, conductivity)
 
     def faces(z):
         here = [cond[s, z, LO:HI, :] for s in range(2)]
@@ -291,7 +300,7 @@
             inv[s, z, LO:HI, :] = i
             zpre[s, z, LO:HI, :] = i * fin[1, s, z, LO:HI, :]
 
-    loop(4, 28, faces)
+    loop(7, 25, faces)
 
     def off_diagonal(field, z, lo, n, sides):
         here = [field[s, z, lo : lo + n, :] for s in range(2)]
@@ -331,6 +340,11 @@
     ex2 = Exchange(sizes, cin, (CZ, PAD, 6), (CX, PAD, 6), 16, pks2, pkr2, ssems.at[1], rsems.at[1], span)
     ex2.pack()
     ex2.start()
+    ex1.unpack(3, 5)
+    loop(3, 6, conductivity)
+    loop(26, 29, conductivity)
+    loop(4, 7, faces)
+    loop(25, 28, faces)
     ex2.wait()
     ex2.unpack()
 
@@ -415,7 +429,7 @@
                 fin[1, s, z, LO:HI, :] + b[s]
             )
 
-    loop(5, 27, post)
+    loop(6, 26, post)
 
     def image(z):
         b = off_diagonal(z0, z, LO, WIN, 2)
@@ -424,7 +438,7 @@
             q0[s, z, LO:HI, :] = q
             zpre[s, z, LO:HI, :] = inv[s, z, LO:HI, :] * q
 
-    loop(6, 26, image)
+    loop(7, 25, image)
 
     for k in range(CZ // 2):
         r = [
@@ -442,8 +456,12 @@
         lz[0, 0, z, own, :] = z0[0, z, own, :]
     ex4 = Exchange(sizes, lz, (NZ, PAD, 4), (NX, PAD, 4), 8, pks4, pkr4, ssems.at[3], rsems.at[3], span)
     ex4.pack()
+    ex4.start()
+    for z in (5, 26):
+        post(z)
+    for z in (6, 25):
+        image(z)
     ex3.wait()
-    ex4.start()
     ex3.unpack()
 
     def first_correction(v2):
@@ -466,7 +484,15 @@
                 q0[s, z, LO:HI, :] + b[s]
             )
 
-    loop(7, 25, post_second)
+    loop(8, 24, post_second)
+
+    for z in range(PAD, PAD + NZ):
+        lw[0, 0, z, own, :] = ww[0, z, own, :] - z0[0, z, own, :]
+    ex5 = Exchange(sizes, lw, (NZ, PAD, 4), (NX, PAD, 4), 8, pks5, pkr5, ssems.at[4], rsems.at[4], span)
+    ex5.pack()
+    ex5.start()
+    for z in (7, 24):
+        post_second(z)
 
     def dots(z, acc):
         w = ww[0, z, own, :]
@@ -474,7 +500,6 @@
         q = q0[0, z, own, :]
         r = fin[1, 0, z, own, :]
         p = diag[0, z, own, :] * w - off_diagonal(ww, z, PAD, NX, 1)[0]
-        lw[0, 0, z, own, :] = w
         terms = (r * zz, zz * q, r * w, q * w, zz * p, w * p)
         return tuple(a + t[0:8] + t[8:16] for a, t in zip(acc, terms))
 
@@ -510,18 +535,105 @@
             values = [a + b for a, b in zip(values[0::2], values[1::2])]
         return values[0]
 
+    wlane = lane_iota(WIN)
+    wrow = lax.broadcasted_iota(jnp.int32, (WIN, LANES), 0) + LO - PAD + gx * NX
+    outside_row = jnp.where(wrow == 0, 1.0, 0.0) + jnp.where(wrow == gxs * NX - 1, 1.0, 0.0)
+    outside_main = outside_row + jnp.where((wlane == 0) & (gy == 0), 1.0, 0.0)
+    outside_main = outside_main + jnp.where((wlane == LANES - 1) & (gy == gys - 1), 1.0, 0.0)
+    outside = (outside_main, outside_row)
+    weight = FILTER_WEIGHT / (1.0 + 6.0 * FILTER_WEIGHT)
+    rest = 1.0 / (1.0 + 6.0 * FILTER_WEIGHT)
+
+    def masked(src, dst):
+        def body(z):
+            inside = plane_in(z, NZ)
+            for s in range(2):
+                dst[s, z, LO:HI, :] = src[0, s, z, LO:HI, :] * (mask[s, LO:HI, :] * inside)
+
+        loop(4, 28, body)
+
+    def gaps(field, z):
+        here = [field[s, z, LO:HI, :] for s in range(2)]
+        ahead, behind = lane_neighbours(here[0], here[1], 1)
+        return [
+            (
+                here[s] - field[s, z - 1, LO:HI, :],
+                here[s] - field[s, z + 1, LO:HI, :],
+                here[s] - field[s, z, LO - 1 : HI - 1, :],
+                here[s] - field[s, z, LO + 1 : HI + 1, :],
+                here[s] - ahead[s],
+                here[s] - behind[s],
+            )
+            for s in range(2)
+        ]
+
+    def product(p, q):
+        t = [a * b for a, b in zip(p, q)]
+        return ((t[0] + t[1]) + (t[2] + t[3])) + (t[4] + t[5])
+
+    def blurred(f, z, lo, n, sides, first):
+        here = [f[s, z, lo : lo + n, :] for s in range(2)]
+        ahead, behind = lane_neighbours(here[0], here[1], 1)
+        g = gz * NZ + z - PAD
+        ends = jnp.where((g == 0) | (g == gzs * NZ - 1), 1.0, 0.0).astype(F32)
+        out = []
+        for s in range(sides):
+            t = f[s, z - 1, lo : lo + n, :] + f[s, z + 1, lo : lo + n, :]
+            t = t + (f[s, z, lo - 1 : lo + n - 1, :] + f[s, z, lo + 1 : lo + n + 1, :])
+            t = t + (ahead[s] + behind[s])
+            t = t + (outside[s][lo - LO : lo - LO + n] + ends) * here[s]
+            out.append(rest * first[s, z, lo : lo + n, :] + weight * t)
+        return out
+
+    def filtered(f, one, two, out):
+        def sweep_to(src, dst):
+            def body(z):
+                inside = plane_in(z, NZ)
+                for s, v in enumerate(blurred(src, z, LO, WIN, 2, f)):
+                    dst[s, z, LO:HI, :] = v * (mask[s, LO:HI, :] * inside)
+
+            return body
+
+        loop(6, 26, sweep_to(f, one))
+        loop(7, 25, sweep_to(one, two))
+        for z in range(PAD, PAD + NZ):
+            parts[out, z - PAD] = blurred(two, z, PAD, NX, 1, f)[0]
+
     share(part, red0, lax.rem(gz, 2), [0], peer0, 5)
-    ex5 = Exchange(sizes, lw, (NZ, PAD, 4), (NX, PAD, 4), 8, pks5, pkr5, ssems.at[4], rsems.at[4], span)
-    ex5.pack()
     part = total_of(red0)
     share(part, red1, gy * (gzs // 2) + gz // 2, group1, peer1, 6)
-    ex5.start()
     ex4.wait()
     ex4.unpack()
+    masked(lz, vv)
+
+    def sensitivity(z):
+        d = gaps(vv, z)
+        inside = plane_in(z, NZ)
+        for s in range(2):
+            r = fin[0, s, z, LO:HI, :]
+            k = (r * r) * (mask[s, LO:HI, :] * (inside * (-3.0 * (1.0 - KMIN) * 0.5)))
+            diag[s, z, LO:HI, :] = k
+            z0[s, z, LO:HI, :] = k * product(d[s], d[s])
+
+    loop(5, 27, sensitivity)
+    filtered(z0, q0, ww, 0)
     part = total_of(red1)
     share(part, red2, gx, group2, peer2, 7)
     ex5.wait()
     ex5.unpack()
+    masked(lw, zpre)
+
+    def sensitivity_rest(z):
+        d, e = gaps(vv, z), gaps(zpre, z)
+        for s in range(2):
+            k = diag[s, z, LO:HI, :]
+            kzm[s, z, LO:HI, :] = k * product(d[s], e[s])
+            kym[s, z, LO:HI, :] = k * product(e[s], e[s])
+
+    loop(5, 27, sensitivity_rest)
+    filtered(kzm, kx, kyp, 1)
+    filtered(kym, cond, inv, 2)
+
     total = total_of(red2)
     total = jnp.broadcast_to(jnp.sum(total, axis=1, keepdims=True), (8, LANES))
     rz, zq, rw, qw, zp, wp = (total[i : i + 1, :] for i in range(6))
@@ -530,82 +642,12 @@
     beta = rz1 / rz
     gamma = 1.0 + beta
     a1 = rz1 / (gamma * gamma * zq - a0 * gamma * (zp + qw) + a0 * a0 * wp)
-    c1 = jnp.broadcast_to(a0 + a1 * gamma, (WIN, LANES))
-    c2 = jnp.broadcast_to(-a1 * a0, (WIN, LANES))
-
-    def solution_plane(z):
-        inside = plane_in(z, NZ)
-        for s in range(2):
-            x = c1 * lz[0, s, z, LO:HI, :] + c2 * lw[0, s, z, LO:HI, :]
-            vv[s, z, LO:HI, :] = x * (mask[s, LO:HI, :] * inside)
-
-    loop(4, 28, solution_plane)
-
-    def copy_out(z):
-        out_t[z] = vv[0, z + PAD, own, :]
-
-    loop(0, NZ, copy_out)
-
-    def sensitivity(z):
-        here = [vv[s, z, LO:HI, :] for s in range(2)]
-        ahead, behind = lane_neighbours(here[0], here[1], 1)
-        inside = plane_in(z, NZ)
-        for s in range(2):
-            x = here[s]
-            g = (x - vv[s, z - 1, LO:HI, :]) ** 2 + (x - vv[s, z + 1, LO:HI, :]) ** 2
-            g = g + (x - vv[s, z, LO - 1 : HI - 1, :]) ** 2
-            g = g + (x - vv[s, z, LO + 1 : HI + 1, :]) ** 2
-            g = g + ((x - ahead[s]) ** 2 + (x - behind[s]) ** 2)
-            r = fin[0, s, z, LO:HI, :] * (mask[s, LO:HI, :] * inside)
-            v = (-3.0 * (1.0 - KMIN) * 0.5) * (r * r) * g
-            z0[s, z, LO:HI, :] = v
-            ww[s, z, LO:HI, :] = v * (1.0 / (1.0 + 6.0 * FILTER_WEIGHT))
-
-    loop(5, 27, sensitivity)
-
-    wlane = lane_iota(WIN)
-    wrow = lax.broadcasted_iota(jnp.int32, (WIN, LANES), 0) + LO - PAD + gx * NX
-    outside_row = jnp.where(wrow == 0, 1.0, 0.0) + jnp.where(wrow == gxs * NX - 1, 1.0, 0.0)
-    outside_main = outside_row + jnp.where((wlane == 0) & (gy == 0), 1.0, 0.0)
-    outside_main = outside_main + jnp.where((wlane == LANES - 1) & (gy == gys - 1), 1.0, 0.0)
-    outside = (outside_main, outside_row)
-    weight = FILTER_WEIGHT / (1.0 + 6.0 * FILTER_WEIGHT)
-
-    def blur(f, f_next, first, end):
-        def body(z):
-            here = [f[s, z, LO:HI, :] for s in range(2)]
-            ahead, behind = lane_neighbours(here[0], here[1], 1)
-            inside = plane_in(z, NZ)
-            g = gz * NZ + z - PAD
-            ends = jnp.where((g == 0) | (g == gzs * NZ - 1), 1.0, 0.0).astype(F32)
-            for s in range(2):
-                t = f[s, z - 1, LO:HI, :] + f[s, z + 1, LO:HI, :]
-                t = t + (f[s, z, LO - 1 : HI - 1, :] + f[s, z, LO + 1 : HI + 1, :])
-                t = t + (ahead[s] + behind[s])
-                t = t + (outside[s] + ends) * here[s]
-                f_next[s, z, LO:HI, :] = ww[s, z, LO:HI, :] + t * (
-                    mask[s, LO:HI, :] * (inside * weight)
-                )
-
-        loop(first, end, body)
-
-    blur(z0, q0, 6, 26)
-    blur(q0, z0, 7, 25)
-
-    def blur_out(k):
-        z = k + PAD
-        f = z0
-        here = [f[s, z, own, :] for s in range(2)]
-        ahead, behind = lane_neighbours(here[0], here[1], 1)
-        g = gz * NZ + k
-        ends = jnp.where((g == 0) | (g == gzs * NZ - 1), 1.0, 0.0).astype(F32)
-        t = f[0, z - 1, own, :] + f[0, z + 1, own, :]
-        t = t + (f[0, z, PAD - 1 : PAD + NX - 1, :] + f[0, z, PAD + 1 : PAD + NX + 1, :])
-        t = t + (ahead[0] + behind[0])
-        t = t + (outside[0][PAD - LO : PAD - LO + NX] + ends) * here[0]
-        out_f[k] = ww[0, z, own, :] + t * weight
-
-    loop(0, NZ, blur_out)
+    c1 = jnp.broadcast_to(a0 + a1 * gamma - a1 * a0, (NX, LANES))
+    c2 = jnp.broadcast_to(-a1 * a0, (NX, LANES))
+    f0, f1, f2 = c1 * c1, 2.0 * c1 * c2, c2 * c2
+    for k in range(NZ):
+        out_t[k] = c1 * vv[0, k + PAD, own, :] + c2 * zpre[0, k + PAD, own, :]
+        out_f[k] = (f0 * parts[0, k] + f1 * parts[1, k]) + f2 * parts[2, k]
 
     for ex in (ex1, ex2, ex3, ex4, ex5):
         ex.finish()
@@ -659,6 +701,7 @@
         *packs(1, NX),
         *packs(1, NX),
         *[pltpu.VMEM((c, 8, LANES), F32) for c in counts],
+        pltpu.VMEM((3, NZ, NX, LANES), F32),
         pltpu.VMEM((2048, LANES), F32),
         pltpu.SemaphoreType.DMA((2,)),
         pltpu.SemaphoreType.DMA((8,)),

time: 44.9 us -> 41 us (0.913)
  Pallas kernels: 44.1 us -> 40.3 us
    pallas_call x1, Pallas kernels: 43.4 us -> 39.6 us  [local(): pl.pallas_call(functools.partial(kernel, sizes), out_shape=(shape, shape)...]
where the time goes in v5:
time: 41 us; the launch traced here: 40.9 us
  Pallas kernels  40.3 us (98%)
  between operations  0.64 us (2%)
    pallas_call x1, Pallas kernels, local(): pl.pallas_call(functools.partial(kernel, sizes), out_shape=(shape, shape)...  39.6 us

profile of v5, /device:TPU:1, one launch (start us, length us, event | category | flops | bytes accessed | tf_op | source)
XLA Modules:
  0.0 40.9 jit_solution(13284465090059637737)
XLA Ops:
  0.6 39.6 %heat_sink_step.1 = (f32[16,16,128]{2,1,0:T(8,128)S(1)}, f32[16,16,128]{2,1,0:T(8,128)S(1)}) custom-call(f32[16,16,128]{2,1,0:T(8,128)} %rho_ref.1, f32[16,16,128]{2,1,0:T(8,128)} %src_ref.1), custom_call_target="tpu_custom_call" | custom-call | tf_op jit(solution)/shard_map/heat_sink_step/pallas_call | solution.py:710
  40.2 0.7 %store_outputs.1 = (f32[16,16,128]{2,1,0:T(8,128)}, f32[16,16,128]{2,1,0:T(8,128)}) custom-call(f32[16,16,128]{2,1,0:T(8,128)S(1)} %get-tuple-element.4.t_ref, f32[16,16,128]{2,1,0:T(8,128)S(1)} %get-tuple-element.5.f_ref), custom_call_target="tpu_custom_call" | custom-call | tf_op jit(solution)/shard_map/store_outputs/pallas_call | solution.py:722

commit v6 on v5

--- a/solution.py
+++ b/solution.py
@@ -173,6 +173,7 @@
     lw,
     ww,
     mask,
+    cinc,
     cin,
     cin2,
     rhs,
@@ -187,6 +188,8 @@
     cmask,
     refined,
     tmp,
+    pks0,
+    pkr0,
     pks1,
     pkr1,
     pks2,
@@ -265,6 +268,41 @@
     cmask[0] = jnp.where(crow_in, 1.0, 0.0)
     cmask[1] = jnp.where(cside_in, 1.0, 0.0)
 
+    even8 = (lane_iota(CX) & 1) == 0
+    even24 = (lane_iota(24) & 1) == 0
+
+    def block_rows(total, k):
+        tmp[k] = pair_lanes(total)
+        return tmp[k, pl.ds(0, CX, 2), :] + tmp[k, pl.ds(1, CX, 2), :]
+
+    def pairs_exchange(arr, halo, rows, group, pks, pkr, sem):
+        return Exchange(
+            sizes,
+            arr,
+            (CZ // 2, PAD // 2, halo),
+            (CX, PAD, rows),
+            group,
+            pks,
+            pkr,
+            ssems.at[sem],
+            rsems.at[sem],
+            span,
+        )
+
+    for k in range(CZ // 2):
+        both = []
+        for j in range(2):
+            total = None
+            for z in (PAD + 4 * k + 2 * j, PAD + 4 * k + 2 * j + 1):
+                r = fin[0, 0, z, PAD : PAD + NX, :]
+                c = KMIN + (1.0 - KMIN) * (r * r * r)
+                total = c if total is None else total + c
+            both.append(0.125 * block_rows(total, CZ + 2 * k + j))
+        cinc[0, 0, PAD // 2 + k, PAD : PAD + CX, :] = jnp.where(even8, both[0], both[1])
+    ex0 = pairs_exchange(cinc, 3, 6, 16, pks0, pkr0, 8)
+    ex0.pack()
+    ex0.start()
+
     ex1.wait()
     ex1.unpack(0, 2)
 
@@ -315,13 +353,6 @@
             out.append((t + u) + v)
         return out
 
-    even8 = (lane_iota(CX) & 1) == 0
-    even24 = (lane_iota(24) & 1) == 0
-
-    def block_rows(total, k):
-        tmp[k] = pair_lanes(total)
-        return tmp[k, pl.ds(0, CX, 2), :] + tmp[k, pl.ds(1, CX, 2), :]
-
     def coarse_rhs(load, field, k):
         total = None
         for j in range(2):
@@ -330,14 +361,13 @@
             total = t if total is None else total + t
         return block_rows(total, k)
 
-    for k in range(CZ):
-        z = PAD + 2 * k
-        c = cond[0, z, PAD : PAD + NX, :] + cond[0, z + 1, PAD : PAD + NX, :]
-        c = 0.125 * block_rows(c, CZ + k)
-        r = coarse_rhs(lambda z: fin[1, 0, z, PAD : PAD + NX, :], zpre, k)
-        cin[0, 0, PAD + k, PAD : PAD + CX, :] = jnp.where(even8, c, r)
-
-    ex2 = Exchange(sizes, cin, (CZ, PAD, 6), (CX, PAD, 6), 16, pks2, pkr2, ssems.at[1], rsems.at[1], span)
+    def coarse_rhs_pairs(load, field, dest):
+        for k in range(CZ // 2):
+            r = [coarse_rhs(load, field, 2 * k + j) for j in range(2)]
+            dest[0, 0, PAD // 2 + k, PAD : PAD + CX, :] = jnp.where(even8, r[0], r[1])
+
+    coarse_rhs_pairs(lambda z: fin[1, 0, z, PAD : PAD + NX, :], zpre, cin)
+    ex2 = pairs_exchange(cin, 3, 5, 16, pks2, pkr2, 1)
     ex2.pack()
     ex2.start()
     ex1.unpack(3, 5)
@@ -345,8 +375,8 @@
     loop(26, 29, conductivity)
     loop(4, 7, faces)
     loop(25, 28, faces)
-    ex2.wait()
-    ex2.unpack()
+    ex0.wait()
+    ex0.unpack()
 
     def split(v):
         return (
@@ -354,14 +384,14 @@
             jnp.where(even24, pltpu.roll(v, LANES - 1, 1), v),
         )
 
-    def coarse_masked(vc):
-        inside = plane_in(vc, CZ)
-        for s in range(2):
-            c, r = split(cin[0, s, vc, 0:24, :])
-            cc[s, vc, 0:24, :] = jnp.where(cmask[s, 0:24, :] * inside > 0.5, c, 0.0)
-            rhs[s, vc, 0:24, :] = r
-
-    loop(2, 22, coarse_masked)
+    def coarse_masked(v2):
+        for s in range(2):
+            for j, c in enumerate(split(cinc[0, s, v2, 0:24, :])):
+                vc = 2 * v2 + j
+                ok = cmask[s, 0:24, :] * plane_in(vc, CZ) > 0.5
+                cc[s, vc, 0:24, :] = jnp.where(ok, c, 0.0)
+
+    loop(1, 11, coarse_masked)
 
     def coarse_faces(vc):
         lo, hi = 3, 27
@@ -383,9 +413,18 @@
             d = (zm + zp) + (xm + xp) + (yp + ym)
             i = jnp.where(cmask[s, lo:hi, :] * inside > 0.5, OMEGA / d, 0.0)
             cinv[s, vc, lo:hi, :] = i
-            ea[s, vc, lo:hi, :] = i * rhs[s, vc, lo:hi, :]
 
     loop(3, 21, coarse_faces)
+
+    def first_correction(arr, vc):
+        v2, j = divmod(vc, 2)
+        for s in range(2):
+            rhs[s, vc, 0:24, :] = split(arr[0, s, v2, 0:24, :])[j]
+            ea[s, vc, 3:27, :] = cinv[s, vc, 3:27, :] * rhs[s, vc, 3:27, :]
+
+    ex2.wait()
+    ex2.unpack()
+    loop(3, 21, lambda vc: first_correction(cin, vc))
 
     def sweep(e, e_next, first, end):
         lo, hi = CLO, CLO + CWIN
@@ -440,14 +479,8 @@
 
     loop(7, 25, image)
 
-    for k in range(CZ // 2):
-        r = [
-            coarse_rhs(lambda z: q0[0, z, PAD : PAD + NX, :], zpre, 2 * k + j) for j in range(2)
-        ]
-        cin2[0, 0, PAD // 2 + k, PAD : PAD + CX, :] = jnp.where(even8, r[0], r[1])
-    ex3 = Exchange(
-        sizes, cin2, (CZ // 2, PAD // 2, 2), (CX, PAD, 4), 8, pks3, pkr3, ssems.at[2], rsems.at[2], span
-    )
+    coarse_rhs_pairs(lambda z: q0[0, z, PAD : PAD + NX, :], zpre, cin2)
+    ex3 = pairs_exchange(cin2, 2, 4, 8, pks3, pkr3, 2)
     ex3.pack()
     ex3.start()
 
@@ -464,14 +497,7 @@
     ex3.wait()
     ex3.unpack()
 
-    def first_correction(v2):
-        for s in range(2):
-            for j, r in enumerate(split(cin2[0, s, v2, 0:24, :])):
-                vc = 2 * v2 + j
-                rhs[s, vc, 0:24, :] = r
-                ea[s, vc, 3:27, :] = cinv[s, vc, 3:27, :] * rhs[s, vc, 3:27, :]
-
-    loop(2, 10, first_correction)
+    loop(4, 20, lambda vc: first_correction(cin2, vc))
     sweep(ea, eb, 5, 19)
     sweep(eb, ea, 6, 18)
     sweep(ea, eb, 7, 17)
@@ -486,11 +512,6 @@
 
     loop(8, 24, post_second)
 
-    for z in range(PAD, PAD + NZ):
-        lw[0, 0, z, own, :] = ww[0, z, own, :] - z0[0, z, own, :]
-    ex5 = Exchange(sizes, lw, (NZ, PAD, 4), (NX, PAD, 4), 8, pks5, pkr5, ssems.at[4], rsems.at[4], span)
-    ex5.pack()
-    ex5.start()
     for z in (7, 24):
         post_second(z)
 
@@ -600,6 +621,11 @@
             parts[out, z - PAD] = blurred(two, z, PAD, NX, 1, f)[0]
 
     share(part, red0, lax.rem(gz, 2), [0], peer0, 5)
+    for z in range(PAD, PAD + NZ):
+        lw[0, 0, z, own, :] = ww[0, z, own, :] - z0[0, z, own, :]
+    ex5 = Exchange(sizes, lw, (NZ, PAD, 4), (NX, PAD, 4), 8, pks5, pkr5, ssems.at[4], rsems.at[4], span)
+    ex5.pack()
+    ex5.start()
     part = total_of(red0)
     share(part, red1, gy * (gzs // 2) + gz // 2, group1, peer1, 6)
     ex4.wait()
@@ -649,7 +675,7 @@
         out_t[k] = c1 * vv[0, k + PAD, own, :] + c2 * zpre[0, k + PAD, own, :]
         out_f[k] = (f0 * parts[0, k] + f1 * parts[1, k]) + f2 * parts[2, k]
 
-    for ex in (ex1, ex2, ex3, ex4, ex5):
+    for ex in (ex0, ex1, ex2, ex3, ex4, ex5):
         ex.finish()
     for rows, sem in shared:
         wait_rows(span, rows, ssems.at[sem])
@@ -689,12 +715,12 @@
         fine(1),
         fine(),
         pltpu.VMEM((2, FZ, LANES), F32),
-        coarse(1),
-        pltpu.VMEM((1, 2, CZP // 2, 32, LANES), F32),
+        *[pltpu.VMEM((1, 2, CZP // 2, 32, LANES), F32) for _ in range(3)],
         *[coarse() for _ in range(9)],
         pltpu.VMEM((2, 32, LANES), F32),
         pltpu.VMEM((CZP, 2, FZ, LANES), F32),
         pltpu.VMEM((2 * CZ, NX, LANES), F32),
+        *packs(1, CX),
         *packs(2, NX),
         *packs(1, CX),
         *packs(1, CX),
@@ -704,8 +730,8 @@
         pltpu.VMEM((3, NZ, NX, LANES), F32),
         pltpu.VMEM((2048, LANES), F32),
         pltpu.SemaphoreType.DMA((2,)),
-        pltpu.SemaphoreType.DMA((8,)),
-        pltpu.SemaphoreType.DMA((8,)),
+        pltpu.SemaphoreType.DMA((9,)),
+        pltpu.SemaphoreType.DMA((9,)),
     ]
     outs = pl.pallas_call(
         functools.partial(kernel, sizes),

time: 41 us -> 40.2 us (0.980)
  Pallas kernels: 40.3 us -> 39.5 us
    pallas_call x1, Pallas kernels: 39.6 us -> 38.8 us  [local(): pl.pallas_call(functools.partial(kernel, sizes), out_shape=(shape, shape)...]
where the time goes in v6:
time: 40.2 us; the launch traced here: 40.1 us
  Pallas kernels  39.5 us (98%)
  between operations  0.64 us (2%)
    pallas_call x1, Pallas kernels, local(): pl.pallas_call(functools.partial(kernel, sizes), out_shape=(shape, shape)...  38.8 us

profile of v6, /device:TPU:1, one launch (start us, length us, event | category | flops | bytes accessed | tf_op | source)
XLA Modules:
  0.0 40.1 jit_solution(10723883634191345050)
XLA Ops:
  0.6 38.8 %heat_sink_step.1 = (f32[16,16,128]{2,1,0:T(8,128)S(1)}, f32[16,16,128]{2,1,0:T(8,128)S(1)}) custom-call(f32[16,16,128]{2,1,0:T(8,128)} %rho_ref.1, f32[16,16,128]{2,1,0:T(8,128)} %src_ref.1), custom_call_target="tpu_custom_call" | custom-call | tf_op jit(solution)/shard_map/heat_sink_step/pallas_call | solution.py:736
  39.4 0.7 %store_outputs.1 = (f32[16,16,128]{2,1,0:T(8,128)}, f32[16,16,128]{2,1,0:T(8,128)}) custom-call(f32[16,16,128]{2,1,0:T(8,128)S(1)} %get-tuple-element.4.t_ref, f32[16,16,128]{2,1,0:T(8,128)S(1)} %get-tuple-element.5.f_ref), custom_call_target="tpu_custom_call" | custom-call | tf_op jit(solution)/shard_map/store_outputs/pallas_call | solution.py:748

commit v7 on v6

--- a/solution.py
+++ b/solution.py
@@ -494,6 +494,16 @@
         post(z)
     for z in (6, 25):
         image(z)
+    zero = jnp.zeros((8, LANES), F32)
+    early = [zero, zero]
+    for z in range(PAD, PAD + NZ):
+        zz = z0[0, z, own, :]
+        for i, t in enumerate((fin[1, 0, z, own, :] * zz, zz * q0[0, z, own, :])):
+            early[i] = early[i] + t[0:8] + t[8:16]
+    which = lax.broadcasted_iota(jnp.int32, (8, LANES), 0)
+    early_part = zero
+    for i, a in enumerate(early):
+        early_part = jnp.where(which == i, jnp.sum(a, axis=0, keepdims=True), early_part)
     ex3.wait()
     ex3.unpack()
 
@@ -521,16 +531,14 @@
         q = q0[0, z, own, :]
         r = fin[1, 0, z, own, :]
         p = diag[0, z, own, :] * w - off_diagonal(ww, z, PAD, NX, 1)[0]
-        terms = (r * zz, zz * q, r * w, q * w, zz * p, w * p)
+        terms = (r * w, q * w, zz * p, w * p)
         return tuple(a + t[0:8] + t[8:16] for a, t in zip(acc, terms))
 
-    zero = jnp.zeros((8, LANES), F32)
-    acc = (zero,) * 6
+    acc = (zero,) * 4
     for z in range(PAD, PAD + NZ):
         acc = dots(z, acc)
-    which = lax.broadcasted_iota(jnp.int32, (8, LANES), 0)
-    part = zero
-    for i, a in enumerate(acc):
+    part = early_part
+    for i, a in enumerate(acc, 2):
         part = jnp.where(which == i, jnp.sum(a, axis=0, keepdims=True), part)
 
     shared = []

time: 40.2 us -> 40.2 us (level)
  no operation moved by 1% of the time
where the time goes in v7:
time: 40.2 us; the launch traced here: 40.1 us
  Pallas kernels  39.5 us (98%)
  between operations  0.64 us (2%)
    pallas_call x1, Pallas kernels, local(): pl.pallas_call(functools.partial(kernel, sizes), out_shape=(shape, shape)...  38.8 us

profile of v7, /device:TPU:1, one launch (start us, length us, event | category | flops | bytes accessed | tf_op | source)
XLA Modules:
  0.0 40.1 jit_solution(16944096239072912052)
XLA Ops:
  0.6 38.8 %heat_sink_step.1 = (f32[16,16,128]{2,1,0:T(8,128)S(1)}, f32[16,16,128]{2,1,0:T(8,128)S(1)}) custom-call(f32[16,16,128]{2,1,0:T(8,128)} %rho_ref.1, f32[16,16,128]{2,1,0:T(8,128)} %src_ref.1), custom_call_target="tpu_custom_call" | custom-call | tf_op jit(solution)/shard_map/heat_sink_step/pallas_call | solution.py:744
  39.4 0.7 %store_outputs.1 = (f32[16,16,128]{2,1,0:T(8,128)}, f32[16,16,128]{2,1,0:T(8,128)}) custom-call(f32[16,16,128]{2,1,0:T(8,128)S(1)} %get-tuple-element.4.t_ref, f32[16,16,128]{2,1,0:T(8,128)S(1)} %get-tuple-element.5.f_ref), custom_call_target="tpu_custom_call" | custom-call | tf_op jit(solution)/shard_map/store_outputs/pallas_call | solution.py:756
